TPU v7x, 256 devices: a whole 4x4x8 slice. The times are simulated.
256 devices in a mesh: real: 4 (over x_lo, core), space: 64 (over y, z, x_hi).
Axes of the slice: x: 4 (x_hi: 2, x_lo: 2; x = x_hi * 2 + x_lo), y: 4, z: 8, core: 2. Of those that a mesh axis runs over, the one named last changes fastest.
Arguments:
- perm_class: int32 [64, 16, 16, 128], P('space'), may hold values from 0 to 7
- class_values: float32 [8], replicated, may hold values from 0.3 to 10
- well_cells: int32 [64], P('real'), parts along dimension 0, may hold values from 0 to 2097151
- well_rates: float32 [64], P('real'), parts along dimension 0, may hold values from 0.5 to 3
- guess: float32 [256, 16, 16, 128], P(('real', 'space')), parts along dimension 0, may hold values from -4 to 4
Outputs:
- pressure: float32 [256, 16, 16, 128], P(('real', 'space')), parts along dimension 0
- residual: float32 [256, 16, 16, 128], P(('real', 'space')), parts along dimension 0
There are 4 independent parts, one for each index of `real`. A program takes and returns all parts, laid end to end along the dimension named above; an argument that names none is the same for every part. Nothing has to cross between parts.
All inputs are finite; a program needn't handle non-finite values.
Results may differ from a plain program's by a relative error of at most 0.00015.
Values sent between devices are 32-bit elements; how exact they have to be, the bound alone decides.
A program may use at most 128 MiB of HBM per device.

v0:
```python
from functools import partial

import jax
import jax.numpy as jnp
from jax import lax
from jax.sharding import PartitionSpec as P

LEVELS = 3
SWEEPS = 2
CSWEEPS = 6


OMEGA = 0.8


def shifted(shard, axis, by):
    peers = lax.axis_size(axis)
    return lax.ppermute(shard, axis, [(i, (i + by) % peers) for i in range(peers)])


def exchange_faces(values, per_side):
    lower_x = shifted(values[-1:], "space", per_side * per_side)
    upper_x = shifted(values[:1], "space", -per_side * per_side)
    lower_y = shifted(values[:, -1:], "space", per_side)
    upper_y = shifted(values[:, :1], "space", -per_side)
    lower_z = shifted(values[:, :, -1:], "space", 1)
    upper_z = shifted(values[:, :, :1], "space", -1)
    return [
        jnp.concatenate([lower_x, values[:-1]], axis=0),
        jnp.concatenate([values[1:], upper_x], axis=0),
        jnp.concatenate([lower_y, values[:, :-1]], axis=1),
        jnp.concatenate([values[:, 1:], upper_y], axis=1),
        jnp.concatenate([lower_z, values[:, :, :-1]], axis=2),
        jnp.concatenate([values[:, :, 1:], upper_z], axis=2),
    ]


def coefficients(permeab, neighbors, scaling):
    face_coefs = [0.5 * (permeab + beside) for beside in neighbors]
    total_sum = face_coefs[0]
    for number in range(1, 6):
        total_sum = total_sum + face_coefs[number]
    return (face_coefs, scaling * total_sum)


def operate(values, neighbors, face_coefs, scaling):
    total_sum = face_coefs[0] * (values - neighbors[0])
    for number in range(1, 6):
        total_sum = total_sum + face_coefs[number] * (values - neighbors[number])
    return scaling * total_sum


def smooth(values, right_side, face_coefs, diagonal, scaling, neighbour):
    return (
        values
        + OMEGA * (right_side - operate(values, neighbour(values), face_coefs, scaling)) / diagonal
    )


def coarsen(values):
    size_x, size_y, size_z = values.shape
    return values.reshape(size_x // 2, 2, size_y // 2, 2, size_z // 2, 2).mean(axis=(1, 3, 5))


def refine(values):
    return jnp.repeat(jnp.repeat(jnp.repeat(values, 2, axis=0), 2, axis=1), 2, axis=2)


def shards(perm_class, class_values, well_cells, well_rates, guess):
    count_dev = lax.axis_size("space")
    per_side = 2 + 2 * (count_dev // 64)
    my_row = lax.axis_index("space")
    block_no = (my_row + per_side * per_side + per_side + 1) % count_dev
    block_x = block_no // (per_side * per_side)
    block_y = block_no // per_side % per_side
    block_z = block_no % per_side
    classes = perm_class[0]
    width_x, width_y, width_z = classes.shape
    neighbour = partial(exchange_faces, per_side=per_side)
    permeab = jnp.zeros(classes.shape, jnp.float32)
    for number in range(class_values.shape[0]):
        permeab = permeab + jnp.where(classes == number, class_values[number], 0.0)
    row_len = per_side * width_z
    plane = per_side * width_y * row_len
    glob_x = well_cells // plane
    glob_y = well_cells // row_len % (per_side * width_y)
    glob_z = well_cells % row_len
    onehot_x = jnp.where(
        (glob_x - block_x * width_x)[:, None] == jnp.arange(width_x)[None, :],
        well_rates[:, None],
        0.0,
    )
    onehot_y = jnp.where(
        (glob_y - block_y * width_y)[:, None] == jnp.arange(width_y)[None, :], 1.0, 0.0
    ).astype(jnp.float32)
    onehot_z = jnp.where(
        (glob_z - block_z * width_z)[:, None] == jnp.arange(width_z)[None, :], 1.0, 0.0
    ).astype(jnp.float32)
    source = jnp.einsum(
        "wi,wj,wk->ijk", onehot_x, onehot_y, onehot_z, precision=lax.Precision.HIGHEST
    )
    perms = [permeab]
    for level_no in range(LEVELS):
        perms.append(coarsen(perms[-1]))
    top_level = LEVELS
    coefs = [
        coefficients(perms[level_no], neighbour(perms[level_no]), 0.25**level_no)
        for level_no in range(top_level)
    ]
    values = guess[0]
    right_side = source
    stored = []
    rights = []
    for level_no in range(top_level):
        face_coefs, diagonal = coefs[level_no]
        scaling = 0.25**level_no
        if level_no == 0:
            count_sw = SWEEPS
        else:
            values = OMEGA * right_side / diagonal
            count_sw = SWEEPS - 1
        for sweep_no in range(count_sw):
            values = smooth(values, right_side, face_coefs, diagonal, scaling, neighbour)
        leftover = right_side - operate(values, neighbour(values), face_coefs, scaling)
        stored.append(values)
        rights.append(right_side)
        right_side = coarsen(leftover)
    scaling = 0.25**LEVELS
    face_coefs, diagonal = coefficients(perms[LEVELS], neighbour(perms[LEVELS]), scaling)
    correction = OMEGA * right_side / diagonal
    for sweep_no in range(CSWEEPS - 1):
        correction = smooth(correction, right_side, face_coefs, diagonal, scaling, neighbour)
    for level_no in reversed(range(top_level)):
        face_coefs, diagonal = coefs[level_no]
        scaling = 0.25**level_no
        values = stored[level_no] + refine(correction)
        for sweep_no in range(SWEEPS):
            values = smooth(values, rights[level_no], face_coefs, diagonal, scaling, neighbour)
        correction = values
    residual = source - operate(correction, neighbour(correction), coefs[0][0], 1.0)
    return (correction[None], residual[None])


def solution(mesh):
    return jax.shard_map(
        shards,
        mesh=mesh,
        in_specs=(
            P("space", None, None, None),
            P(),
            P("real"),
            P("real"),
            P(("real", "space"), None, None, None),
        ),
        out_specs=(P(("real", "space"), None, None, None), P(("real", "space"), None, None, None)),
        check_vma=False,
    )
```

profile of v0, /device:TPU:2, one launch (start us, length us, event | category | flops | bytes accessed | tf_op | source)
XLA Modules:
  0.0 595.3 jit_solution(18020324032566245876)
XLA Ops:
  16.6 7.6 %collective-permute-start.10 = (f32[16,16,1]{2,0,1:T(8,128)}, f32[16,16,1]{2,0,1:T(8,128)S(1)}, u32[]{:S(2)}, u32[]{:S(2)}) collective-permute-start(f32[16,16,1]{2,0,1:T(8,128)} %get-tuple-element.126), channel_id=1, source_target_pairs={{0,63},{1,0},{2,1},{3,2},{4,3},{5,4},{6,5},{7,6},{8,7},{9,8},{10,9... | collective-permute-start | bytes 3080 | tf_op jit(solution)/shard_map/ppermute | solution.py:18
  28.0 9.8 %reshape.205 = f32[8,2,8,2,64,2]{5,4,3,2,1,0:T(8,128)} reshape(f32[1,16,16,128]{3,2,1,0:T(8,128)S(1)} %add_add_fusion) | data formatting | bytes 262144 | tf_op jit(solution)/shard_map/add | solution.py:82
  60.7 7.3 %collective-permute-done.9 = f32[16,16,1]{2,0,1:T(8,128)} collective-permute-done((f32[16,16,1]{2,0,1:T(8,128)}, f32[16,16,1]{2,0,1:T(8,128)}, u32[]{:S(2)}, u32[]{:S(2)}) %collective-permute-start.9) | collective-permute-done | bytes 1056 | tf_op jit(solution)/shard_map/ppermute | solution.py:18
  93.7 8.8 %collective-permute-done.16 = f32[16,16,1]{2,0,1:T(8,128)S(1)} collective-permute-done((f32[16,16,1]{2,0,1:T(8,128)S(1)}, f32[16,16,1]{2,0,1:T(8,128)S(1)}, u32[]{:S(2)}, u32[]{:S(2)}) %collective-permute-start.16) | collective-permute-done | bytes 1056 | tf_op jit(solution)/shard_map/ppermute | solution.py:18
  113.9 10.5 %collective-permute-done.22 = f32[16,16,1]{2,0,1:T(8,128)S(1)} collective-permute-done((f32[16,16,1]{2,0,1:T(8,128)S(1)}, f32[16,16,1]{2,0,1:T(8,128)S(1)}, u32[]{:S(2)}, u32[]{:S(2)}) %collective-permute-start.22) | collective-permute-done | bytes 1056 | tf_op jit(solution)/shard_map/ppermute | solution.py:18
  131.1 9.8 %reshape.186 = f32[8,2,8,2,64,2]{5,4,3,2,1,0:T(8,128)} reshape(f32[16,16,128]{2,1,0:T(8,128)S(1)} %copy.155) | data formatting | bytes 262144 | tf_op jit(solution)/shard_map/reshape | solution.py:62
  151.6 10.2 %collective-permute-start.35 = (f32[8,8,1]{2,1,0:T(8,128)S(1)}, f32[8,8,1]{2,1,0:T(8,128)S(1)}, u32[]{:S(2)}, u32[]{:S(2)}) collective-permute-start(f32[8,8,1]{2,1,0:T(8,128)S(1)} %get-tuple-element.185), channel_id=1, source_target_pairs={{0,63},{1,0},{2,1},{3,2},{4,3},{5,4},{6,5},{7,6},{8,7},{9,8},{10,9... | collective-permute-start | bytes 776 | tf_op jit(solution)/shard_map/ppermute | solution.py:18
  174.2 6.6 %collective-permute-done.34 = f32[8,8,1]{2,1,0:T(8,128)S(1)} collective-permute-done((f32[8,8,1]{2,1,0:T(8,128)S(1)}, f32[8,8,1]{2,1,0:T(8,128)S(1)}, u32[]{:S(2)}, u32[]{:S(2)}) %collective-permute-start.34) | collective-permute-done | bytes 288 | tf_op jit(solution)/shard_map/ppermute | solution.py:18
  200.0 7.4 %collective-permute-start.41 = (f32[8,8,1]{2,1,0:T(8,128)}, f32[8,8,1]{2,1,0:T(8,128)S(1)}, u32[]{:S(2)}, u32[]{:S(2)}) collective-permute-start(f32[8,8,1]{2,1,0:T(8,128)} %get-tuple-element.180), channel_id=1, source_target_pairs={{0,63},{1,0},{2,1},{3,2},{4,3},{5,4},{6,5},{7,6},{8,7},{9,8},{10,9... | collective-permute-start | bytes 776 | tf_op jit(solution)/shard_map/ppermute | solution.py:18
  213.1 8.0 %collective-permute-done.38 = f32[8,1,64]{2,1,0:T(1,128)S(1)} collective-permute-done((f32[8,1,64]{2,1,0:T(1,128)}, f32[8,1,64]{2,1,0:T(1,128)S(1)}, u32[]{:S(2)}, u32[]{:S(2)}) %collective-permute-start.38) | collective-permute-done | bytes 2080 | tf_op jit(solution)/shard_map/ppermute | solution.py:18
  234.9 9.1 %collective-permute-start.47 = (f32[4,4,1]{2,1,0:T(4,128)S(1)}, f32[4,4,1]{2,1,0:T(4,128)S(1)}, u32[]{:S(2)}, u32[]{:S(2)}) collective-permute-start(f32[4,4,1]{2,1,0:T(4,128)S(1)} %copy-done.28), channel_id=1, source_target_pairs={{0,63},{1,0},{2,1},{3,2},{4,3},{5,4},{6,5},{7,6},{8,7},{9,8},{10,9... | collective-permute-start | bytes 200 | tf_op jit(solution)/shard_map/ppermute | solution.py:18
  248.3 8.3 %collective-permute-done.46 = f32[4,4,1]{2,1,0:T(4,128)S(1)} collective-permute-done((f32[4,4,1]{2,1,0:T(4,128)}, f32[4,4,1]{2,1,0:T(4,128)S(1)}, u32[]{:S(2)}, u32[]{:S(2)}) %collective-permute-start.46) | collective-permute-done | bytes 96 | tf_op jit(solution)/shard_map/ppermute | solution.py:18
  283.5 8.6 %collective-permute-done.58 = f32[4,4,1]{2,1,0:T(4,128)S(1)} collective-permute-done((f32[4,4,1]{2,1,0:T(4,128)S(1)}, f32[4,4,1]{2,1,0:T(4,128)S(1)}, u32[]{:S(2)}, u32[]{:S(2)}) %collective-permute-start.58) | collective-permute-done | bytes 96 | tf_op jit(solution)/shard_map/ppermute | solution.py:18
  301.5 7.2 %collective-permute-done.56 = f32[4,1,32]{2,1,0:T(1,128)S(1)} collective-permute-done((f32[4,1,32]{2,1,0:T(1,128)S(1)}, f32[4,1,32]{2,1,0:T(1,128)S(1)}, u32[]{:S(2)}, u32[]{:S(2)}) %collective-permute-start.56) | collective-permute-done | bytes 544 | tf_op jit(solution)/shard_map/ppermute | solution.py:18
  327.2 9.5 %collective-permute-done.64 = f32[2,2,1]{2,1,0:T(2,128)S(1)} collective-permute-done((f32[2,2,1]{2,1,0:T(2,128)}, f32[2,2,1]{2,1,0:T(2,128)S(1)}, u32[]{:S(2)}, u32[]{:S(2)}) %collective-permute-start.64) | collective-permute-done | bytes 48 | tf_op jit(solution)/shard_map/ppermute | solution.py:18
  341.0 6.2 %collective-permute-start.69 = (f32[2,1,16]{2,1,0:T(1,128)S(1)}, f32[2,1,16]{2,1,0:T(1,128)S(1)}, u32[]{:S(2)}, u32[]{:S(2)}) collective-permute-start(f32[2,1,16]{2,1,0:T(1,128)S(1)} %get-tuple-element.306), channel_id=1, source_target_pairs={{0,60},{1,61},{2,62},{3,63},{4,0},{5,1},{6,2},{7,3},{8,4},{9,5},{1... | collective-permute-start | bytes 392 | tf_op jit(solution)/shard_map/ppermute | solution.py:18
  347.4 9.3 %collective-permute-done.70 = f32[2,2,1]{2,1,0:T(2,128)S(1)} collective-permute-done((f32[2,2,1]{2,1,0:T(2,128)S(1)}, f32[2,2,1]{2,1,0:T(2,128)S(1)}, u32[]{:S(2)}, u32[]{:S(2)}) %collective-permute-start.70) | collective-permute-done | bytes 48 | tf_op jit(solution)/shard_map/ppermute | solution.py:18
  365.3 6.2 %collective-permute-start.75 = (f32[2,1,16]{2,1,0:T(1,128)S(1)}, f32[2,1,16]{2,1,0:T(1,128)S(1)}, u32[]{:S(2)}, u32[]{:S(2)}) collective-permute-start(f32[2,1,16]{2,1,0:T(1,128)S(1)} %get-tuple-element.298), channel_id=1, source_target_pairs={{0,60},{1,61},{2,62},{3,63},{4,0},{5,1},{6,2},{7,3},{8,4},{9,5},{1... | collective-permute-start | bytes 392 | tf_op jit(solution)/shard_map/ppermute | solution.py:18
  371.6 9.3 %collective-permute-done.76 = f32[2,2,1]{2,1,0:T(2,128)S(1)} collective-permute-done((f32[2,2,1]{2,1,0:T(2,128)S(1)}, f32[2,2,1]{2,1,0:T(2,128)S(1)}, u32[]{:S(2)}, u32[]{:S(2)}) %collective-permute-start.76) | collective-permute-done | bytes 48 | tf_op jit(solution)/shard_map/ppermute | solution.py:18
  389.5 6.2 %collective-permute-start.81 = (f32[2,1,16]{2,1,0:T(1,128)S(1)}, f32[2,1,16]{2,1,0:T(1,128)S(1)}, u32[]{:S(2)}, u32[]{:S(2)}) collective-permute-start(f32[2,1,16]{2,1,0:T(1,128)S(1)} %get-tuple-element.290), channel_id=1, source_target_pairs={{0,60},{1,61},{2,62},{3,63},{4,0},{5,1},{6,2},{7,3},{8,4},{9,5},{1... | collective-permute-start | bytes 392 | tf_op jit(solution)/shard_map/ppermute | solution.py:18
  395.7 9.3 %collective-permute-done.82 = f32[2,2,1]{2,1,0:T(2,128)S(1)} collective-permute-done((f32[2,2,1]{2,1,0:T(2,128)S(1)}, f32[2,2,1]{2,1,0:T(2,128)S(1)}, u32[]{:S(2)}, u32[]{:S(2)}) %collective-permute-start.82) | collective-permute-done | bytes 48 | tf_op jit(solution)/shard_map/ppermute | solution.py:18
  414.0 6.2 %collective-permute-start.87 = (f32[2,1,16]{2,1,0:T(1,128)S(1)}, f32[2,1,16]{2,1,0:T(1,128)S(1)}, u32[]{:S(2)}, u32[]{:S(2)}) collective-permute-start(f32[2,1,16]{2,1,0:T(1,128)S(1)} %get-tuple-element.282), channel_id=1, source_target_pairs={{0,60},{1,61},{2,62},{3,63},{4,0},{5,1},{6,2},{7,3},{8,4},{9,5},{1... | collective-permute-start | bytes 392 | tf_op jit(solution)/shard_map/ppermute | solution.py:18
  420.3 9.3 %collective-permute-done.88 = f32[2,2,1]{2,1,0:T(2,128)S(1)} collective-permute-done((f32[2,2,1]{2,1,0:T(2,128)S(1)}, f32[2,2,1]{2,1,0:T(2,128)S(1)}, u32[]{:S(2)}, u32[]{:S(2)}) %collective-permute-start.88) | collective-permute-done | bytes 48 | tf_op jit(solution)/shard_map/ppermute | solution.py:18
  438.2 6.3 %collective-permute-start.93 = (f32[2,1,16]{2,1,0:T(1,128)S(1)}, f32[2,1,16]{2,1,0:T(1,128)S(1)}, u32[]{:S(2)}, u32[]{:S(2)}) collective-permute-start(f32[2,1,16]{2,1,0:T(1,128)S(1)} %get-tuple-element.274), channel_id=1, source_target_pairs={{0,60},{1,61},{2,62},{3,63},{4,0},{5,1},{6,2},{7,3},{8,4},{9,5},{1... | collective-permute-start | bytes 392 | tf_op jit(solution)/shard_map/ppermute | solution.py:18
  444.4 9.3 %collective-permute-done.94 = f32[2,2,1]{2,1,0:T(2,128)S(1)} collective-permute-done((f32[2,2,1]{2,1,0:T(2,128)S(1)}, f32[2,2,1]{2,1,0:T(2,128)S(1)}, u32[]{:S(2)}, u32[]{:S(2)}) %collective-permute-start.94) | collective-permute-done | bytes 48 | tf_op jit(solution)/shard_map/ppermute | solution.py:18
  462.6 6.2 %collective-permute-start.99 = (f32[4,1,32]{2,1,0:T(1,128)S(1)}, f32[4,1,32]{2,1,0:T(1,128)S(1)}, u32[]{:S(2)}, u32[]{:S(2)}) collective-permute-start(f32[4,1,32]{2,1,0:T(1,128)S(1)} %get-tuple-element.224), channel_id=1, source_target_pairs={{0,60},{1,61},{2,62},{3,63},{4,0},{5,1},{6,2},{7,3},{8,4},{9,5},{1... | collective-permute-start | bytes 1544 | tf_op jit(solution)/shard_map/ppermute | solution.py:18
  481.7 6.2 %collective-permute-start.105 = (f32[4,1,32]{2,1,0:T(1,128)S(1)}, f32[4,1,32]{2,1,0:T(1,128)S(1)}, u32[]{:S(2)}, u32[]{:S(2)}) collective-permute-start(f32[4,1,32]{2,1,0:T(1,128)S(1)} %get-tuple-element.212), channel_id=1, source_target_pairs={{0,60},{1,61},{2,62},{3,63},{4,0},{5,1},{6,2},{7,3},{8,4},{9,5},{1... | collective-permute-start | bytes 1544 | tf_op jit(solution)/shard_map/ppermute | solution.py:18
  508.1 9.6 %collective-permute-done.112 = f32[8,8,1]{2,1,0:T(8,128)S(1)} collective-permute-done((f32[8,8,1]{2,1,0:T(8,128)S(1)}, f32[8,8,1]{2,1,0:T(8,128)S(1)}, u32[]{:S(2)}, u32[]{:S(2)}) %collective-permute-start.112) | collective-permute-done | bytes 288 | tf_op jit(solution)/shard_map/ppermute | solution.py:18
  527.6 8.1 %collective-permute-done.118 = f32[8,8,1]{2,1,0:T(8,128)S(1)} collective-permute-done((f32[8,8,1]{2,1,0:T(8,128)S(1)}, f32[8,8,1]{2,1,0:T(8,128)S(1)}, u32[]{:S(2)}, u32[]{:S(2)}) %collective-permute-start.118) | collective-permute-done | bytes 288 | tf_op jit(solution)/shard_map/ppermute | solution.py:18
  546.4 8.7 %collective-permute-done.124 = f32[16,16,1]{2,0,1:T(8,128)S(1)} collective-permute-done((f32[16,16,1]{2,0,1:T(8,128)S(1)}, f32[16,16,1]{2,0,1:T(8,128)S(1)}, u32[]{:S(2)}, u32[]{:S(2)}) %collective-permute-start.124) | collective-permute-done | bytes 1056 | tf_op jit(solution)/shard_map/ppermute | solution.py:18
  564.2 9.7 %collective-permute-done.130 = f32[16,16,1]{2,0,1:T(8,128)S(1)} collective-permute-done((f32[16,16,1]{2,0,1:T(8,128)S(1)}, f32[16,16,1]{2,0,1:T(8,128)S(1)}, u32[]{:S(2)}, u32[]{:S(2)}) %collective-permute-start.130) | collective-permute-done | bytes 1056 | tf_op jit(solution)/shard_map/ppermute | solution.py:18
  583.9 10.0 %collective-permute-done.136 = f32[16,16,1]{2,0,1:T(8,128)S(1)} collective-permute-done((f32[16,16,1]{2,0,1:T(8,128)S(1)}, f32[16,16,1]{2,0,1:T(8,128)S(1)}, u32[]{:S(2)}, u32[]{:S(2)}) %collective-permute-start.136) | collective-permute-done | bytes 1056 | tf_op jit(solution)/shard_map/ppermute | solution.py:18
  (579 shorter events, 327.4 us)
Async XLA Ops:
  2.0 66.0 %collective-permute-start.1 = (f32[1,16,128]{2,0,1:T(1,128)}, f32[1,16,128]{2,0,1:T(1,128)S(1)}, u32[]{:S(2)}, u32[]{:S(2)}) collective-permute-start(f32[1,16,128]{2,0,1:T(1,128)} %bitcast.15), channel_id=1, source_target_pairs={{0,16},{1,17},{2,18},{3,19},{4,20},{5,21},{6,22},{7,23},{8,24},{9,... | collective-permute-start | bytes 24584 | tf_op jit(solution)/shard_map/ppermute | solution.py:18
  3.5 67.4 %collective-permute-start.3 = (f32[1,16,128]{2,0,1:T(1,128)}, f32[1,16,128]{2,0,1:T(1,128)}, u32[]{:S(2)}, u32[]{:S(2)}) collective-permute-start(f32[1,16,128]{2,0,1:T(1,128)} %bitcast.20), channel_id=1, source_target_pairs={{0,48},{1,49},{2,50},{3,51},{4,52},{5,53},{6,54},{7,55},{8,56},{9,... | collective-permute-start | bytes 24584 | tf_op jit(solution)/shard_map/ppermute | solution.py:18
  13.3 57.8 %collective-permute-start = (f32[1,16,128]{2,1,0:T(8,128)}, f32[1,16,128]{2,1,0:T(8,128)}, u32[]{:S(2)}, u32[]{:S(2)}) collective-permute-start(f32[1,16,128]{2,1,0:T(8,128)} %get-tuple-element.120), channel_id=1, source_target_pairs={{0,16},{1,17},{2,18},{3,19},{4,20},{5,21},{6,22},{7,23},{8,24},{9,... | collective-permute-start | bytes 24584 | tf_op jit(solution)/shard_map/ppermute | solution.py:18
  14.4 39.0 %collective-permute-start.8 = (f32[16,16,1]{2,0,1:T(8,128)S(1)}, f32[16,16,1]{2,0,1:T(8,128)S(1)}, u32[]{:S(2)}, u32[]{:S(2)}) collective-permute-start(f32[16,16,1]{2,0,1:T(8,128)S(1)} %get-tuple-element.125), channel_id=1, source_target_pairs={{0,1},{1,2},{2,3},{3,4},{4,5},{5,6},{6,7},{7,8},{8,9},{9,10},{10,1... | collective-permute-start | bytes 3080 | tf_op jit(solution)/shard_map/ppermute | solution.py:18
  16.6 40.4 %collective-permute-start.10 = (f32[16,16,1]{2,0,1:T(8,128)}, f32[16,16,1]{2,0,1:T(8,128)S(1)}, u32[]{:S(2)}, u32[]{:S(2)}) collective-permute-start(f32[16,16,1]{2,0,1:T(8,128)} %get-tuple-element.126), channel_id=1, source_target_pairs={{0,63},{1,0},{2,1},{3,2},{4,3},{5,4},{6,5},{7,6},{8,7},{9,8},{10,9... | collective-permute-start | bytes 3080 | tf_op jit(solution)/shard_map/ppermute | solution.py:18
  60.1 22.9 %collective-permute-start.2 = (f32[1,16,128]{2,0,1:T(1,128)}, f32[1,16,128]{2,0,1:T(1,128)S(1)}, u32[]{:S(2)}, u32[]{:S(2)}) collective-permute-start(f32[1,16,128]{2,0,1:T(1,128)} %bitcast.18), channel_id=1, source_target_pairs={{0,48},{1,49},{2,50},{3,51},{4,52},{5,53},{6,54},{7,55},{8,56},{9,... | collective-permute-start | bytes 24584 | tf_op jit(solution)/shard_map/ppermute | solution.py:18
  107.0 20.9 %collective-permute-start.18 = (f32[1,16,128]{2,0,1:T(1,128)S(1)}, f32[1,16,128]{2,0,1:T(1,128)S(1)}, u32[]{:S(2)}, u32[]{:S(2)}) collective-permute-start(f32[1,16,128]{2,0,1:T(1,128)S(1)} %get-tuple-element.104), channel_id=1, source_target_pairs={{0,16},{1,17},{2,18},{3,19},{4,20},{5,21},{6,22},{7,23},{8,24},{9,... | collective-permute-start | bytes 24584 | tf_op jit(solution)/shard_map/ppermute | solution.py:18
  109.0 21.8 %collective-permute-start.20 = (f32[16,1,128]{2,0,1:T(8,128)S(1)}, f32[16,1,128]{2,0,1:T(8,128)S(1)}, u32[]{:S(2)}, u32[]{:S(2)}) collective-permute-start(f32[16,1,128]{2,0,1:T(8,128)S(1)} %get-tuple-element.100), channel_id=1, source_target_pairs={{0,4},{1,5},{2,6},{3,7},{4,8},{5,9},{6,10},{7,11},{8,12},{9,13},{1... | collective-permute-start | bytes 24584 | tf_op jit(solution)/shard_map/ppermute | solution.py:18
  145.4 35.4 %collective-permute-start.30 = (f32[1,8,64]{2,1,0:T(8,128)S(1)}, f32[1,8,64]{2,1,0:T(8,128)S(1)}, u32[]{:S(2)}, u32[]{:S(2)}) collective-permute-start(f32[1,8,64]{2,1,0:T(8,128)S(1)} %get-tuple-element.191), channel_id=1, source_target_pairs={{0,16},{1,17},{2,18},{3,19},{4,20},{5,21},{6,22},{7,23},{8,24},{9,... | collective-permute-start | bytes 6152 | tf_op jit(solution)/shard_map/ppermute | solution.py:18
  145.4 38.6 %collective-permute-start.31 = (f32[1,8,64]{2,1,0:T(8,128)S(1)}, f32[1,8,64]{2,1,0:T(8,128)S(1)}, u32[]{:S(2)}, u32[]{:S(2)}) collective-permute-start(f32[1,8,64]{2,1,0:T(8,128)S(1)} %get-tuple-element.192), channel_id=1, source_target_pairs={{0,48},{1,49},{2,50},{3,51},{4,52},{5,53},{6,54},{7,55},{8,56},{9,... | collective-permute-start | bytes 6152 | tf_op jit(solution)/shard_map/ppermute | solution.py:18
  148.6 35.3 %collective-permute-start.33 = (f32[8,1,64]{2,1,0:T(1,128)S(1)}, f32[8,1,64]{2,1,0:T(1,128)S(1)}, u32[]{:S(2)}, u32[]{:S(2)}) collective-permute-start(f32[8,1,64]{2,1,0:T(1,128)S(1)} %get-tuple-element.189), channel_id=1, source_target_pairs={{0,60},{1,61},{2,62},{3,63},{4,0},{5,1},{6,2},{7,3},{8,4},{9,5},{1... | collective-permute-start | bytes 6152 | tf_op jit(solution)/shard_map/ppermute | solution.py:18
  150.9 36.1 %collective-permute-start.32 = (f32[8,1,64]{2,1,0:T(1,128)S(1)}, f32[8,1,64]{2,1,0:T(1,128)S(1)}, u32[]{:S(2)}, u32[]{:S(2)}) collective-permute-start(f32[8,1,64]{2,1,0:T(1,128)S(1)} %get-tuple-element.190), channel_id=1, source_target_pairs={{0,4},{1,5},{2,6},{3,7},{4,8},{5,9},{6,10},{7,11},{8,12},{9,13},{1... | collective-permute-start | bytes 6152 | tf_op jit(solution)/shard_map/ppermute | solution.py:18
  180.7 75.8 %collective-permute-start.42 = (f32[1,4,32]{2,1,0:T(4,128)}, f32[1,4,32]{2,1,0:T(4,128)}, u32[]{:S(2)}, u32[]{:S(2)}) collective-permute-start(f32[1,4,32]{2,1,0:T(4,128)} %get-tuple-element.267), channel_id=1, source_target_pairs={{0,16},{1,17},{2,18},{3,19},{4,20},{5,21},{6,22},{7,23},{8,24},{9,... | collective-permute-start | bytes 1544 | tf_op jit(solution)/shard_map/ppermute | solution.py:18
  180.7 75.8 %collective-permute-start.43 = (f32[1,4,32]{2,1,0:T(4,128)}, f32[1,4,32]{2,1,0:T(4,128)}, u32[]{:S(2)}, u32[]{:S(2)}) collective-permute-start(f32[1,4,32]{2,1,0:T(4,128)} %get-tuple-element.268), channel_id=1, source_target_pairs={{0,48},{1,49},{2,50},{3,51},{4,52},{5,53},{6,54},{7,55},{8,56},{9,... | collective-permute-start | bytes 1544 | tf_op jit(solution)/shard_map/ppermute | solution.py:18
  184.0 72.6 %collective-permute-start.45 = (f32[4,1,32]{2,1,0:T(1,128)}, f32[4,1,32]{2,1,0:T(1,128)}, u32[]{:S(2)}, u32[]{:S(2)}) collective-permute-start(f32[4,1,32]{2,1,0:T(1,128)} %get-tuple-element.265), channel_id=1, source_target_pairs={{0,60},{1,61},{2,62},{3,63},{4,0},{5,1},{6,2},{7,3},{8,4},{9,5},{1... | collective-permute-start | bytes 1544 | tf_op jit(solution)/shard_map/ppermute | solution.py:18
  184.0 72.6 %collective-permute-start.44 = (f32[4,1,32]{2,1,0:T(1,128)}, f32[4,1,32]{2,1,0:T(1,128)}, u32[]{:S(2)}, u32[]{:S(2)}) collective-permute-start(f32[4,1,32]{2,1,0:T(1,128)} %get-tuple-element.266), channel_id=1, source_target_pairs={{0,4},{1,5},{2,6},{3,7},{4,8},{5,9},{6,10},{7,11},{8,12},{9,13},{1... | collective-permute-start | bytes 1544 | tf_op jit(solution)/shard_map/ppermute | solution.py:18
  271.4 65.3 %collective-permute-start.60 = (f32[1,2,16]{2,1,0:T(2,128)}, f32[1,2,16]{2,1,0:T(2,128)}, u32[]{:S(2)}, u32[]{:S(2)}) collective-permute-start(f32[1,2,16]{2,1,0:T(2,128)} %get-tuple-element.317), channel_id=1, source_target_pairs={{0,16},{1,17},{2,18},{3,19},{4,20},{5,21},{6,22},{7,23},{8,24},{9,... | collective-permute-start | bytes 392 | tf_op jit(solution)/shard_map/ppermute | solution.py:18
  271.4 65.3 %collective-permute-start.61 = (f32[1,2,16]{2,1,0:T(2,128)}, f32[1,2,16]{2,1,0:T(2,128)}, u32[]{:S(2)}, u32[]{:S(2)}) collective-permute-start(f32[1,2,16]{2,1,0:T(2,128)} %get-tuple-element.318), channel_id=1, source_target_pairs={{0,48},{1,49},{2,50},{3,51},{4,52},{5,53},{6,54},{7,55},{8,56},{9,... | collective-permute-start | bytes 392 | tf_op jit(solution)/shard_map/ppermute | solution.py:18
  274.7 62.1 %collective-permute-start.62 = (f32[2,1,16]{2,1,0:T(1,128)}, f32[2,1,16]{2,1,0:T(1,128)}, u32[]{:S(2)}, u32[]{:S(2)}) collective-permute-start(f32[2,1,16]{2,1,0:T(1,128)} %get-tuple-element.315), channel_id=1, source_target_pairs={{0,4},{1,5},{2,6},{3,7},{4,8},{5,9},{6,10},{7,11},{8,12},{9,13},{1... | collective-permute-start | bytes 392 | tf_op jit(solution)/shard_map/ppermute | solution.py:18
  275.1 61.6 %collective-permute-start.63 = (f32[2,1,16]{2,1,0:T(1,128)}, f32[2,1,16]{2,1,0:T(1,128)}, u32[]{:S(2)}, u32[]{:S(2)}) collective-permute-start(f32[2,1,16]{2,1,0:T(1,128)} %get-tuple-element.316), channel_id=1, source_target_pairs={{0,60},{1,61},{2,62},{3,63},{4,0},{5,1},{6,2},{7,3},{8,4},{9,5},{1... | collective-permute-start | bytes 392 | tf_op jit(solution)/shard_map/ppermute | solution.py:18
  337.8 24.0 %collective-permute-start.66 = (f32[1,2,16]{2,1,0:T(2,128)S(1)}, f32[1,2,16]{2,1,0:T(2,128)S(1)}, u32[]{:S(2)}, u32[]{:S(2)}) collective-permute-start(f32[1,2,16]{2,1,0:T(2,128)S(1)} %get-tuple-element.303), channel_id=1, source_target_pairs={{0,16},{1,17},{2,18},{3,19},{4,20},{5,21},{6,22},{7,23},{8,24},{9,... | collective-permute-start | bytes 392 | tf_op jit(solution)/shard_map/ppermute | solution.py:18
  337.8 24.0 %collective-permute-start.67 = (f32[1,2,16]{2,1,0:T(2,128)S(1)}, f32[1,2,16]{2,1,0:T(2,128)S(1)}, u32[]{:S(2)}, u32[]{:S(2)}) collective-permute-start(f32[1,2,16]{2,1,0:T(2,128)S(1)} %get-tuple-element.304), channel_id=1, source_target_pairs={{0,48},{1,49},{2,50},{3,51},{4,52},{5,53},{6,54},{7,55},{8,56},{9,... | collective-permute-start | bytes 392 | tf_op jit(solution)/shard_map/ppermute | solution.py:18
  341.0 20.8 %collective-permute-start.69 = (f32[2,1,16]{2,1,0:T(1,128)S(1)}, f32[2,1,16]{2,1,0:T(1,128)S(1)}, u32[]{:S(2)}, u32[]{:S(2)}) collective-permute-start(f32[2,1,16]{2,1,0:T(1,128)S(1)} %get-tuple-element.306), channel_id=1, source_target_pairs={{0,60},{1,61},{2,62},{3,63},{4,0},{5,1},{6,2},{7,3},{8,4},{9,5},{1... | collective-permute-start | bytes 392 | tf_op jit(solution)/shard_map/ppermute | solution.py:18
  362.1 23.9 %collective-permute-start.72 = (f32[1,2,16]{2,1,0:T(2,128)S(1)}, f32[1,2,16]{2,1,0:T(2,128)S(1)}, u32[]{:S(2)}, u32[]{:S(2)}) collective-permute-start(f32[1,2,16]{2,1,0:T(2,128)S(1)} %get-tuple-element.295), channel_id=1, source_target_pairs={{0,16},{1,17},{2,18},{3,19},{4,20},{5,21},{6,22},{7,23},{8,24},{9,... | collective-permute-start | bytes 392 | tf_op jit(solution)/shard_map/ppermute | solution.py:18
  362.1 23.9 %collective-permute-start.73 = (f32[1,2,16]{2,1,0:T(2,128)S(1)}, f32[1,2,16]{2,1,0:T(2,128)S(1)}, u32[]{:S(2)}, u32[]{:S(2)}) collective-permute-start(f32[1,2,16]{2,1,0:T(2,128)S(1)} %get-tuple-element.296), channel_id=1, source_target_pairs={{0,48},{1,49},{2,50},{3,51},{4,52},{5,53},{6,54},{7,55},{8,56},{9,... | collective-permute-start | bytes 392 | tf_op jit(solution)/shard_map/ppermute | solution.py:18
  386.2 23.9 %collective-permute-start.78 = (f32[1,2,16]{2,1,0:T(2,128)S(1)}, f32[1,2,16]{2,1,0:T(2,128)S(1)}, u32[]{:S(2)}, u32[]{:S(2)}) collective-permute-start(f32[1,2,16]{2,1,0:T(2,128)S(1)} %get-tuple-element.287), channel_id=1, source_target_pairs={{0,16},{1,17},{2,18},{3,19},{4,20},{5,21},{6,22},{7,23},{8,24},{9,... | collective-permute-start | bytes 392 | tf_op jit(solution)/shard_map/ppermute | solution.py:18
  386.2 23.9 %collective-permute-start.79 = (f32[1,2,16]{2,1,0:T(2,128)S(1)}, f32[1,2,16]{2,1,0:T(2,128)S(1)}, u32[]{:S(2)}, u32[]{:S(2)}) collective-permute-start(f32[1,2,16]{2,1,0:T(2,128)S(1)} %get-tuple-element.288), channel_id=1, source_target_pairs={{0,48},{1,49},{2,50},{3,51},{4,52},{5,53},{6,54},{7,55},{8,56},{9,... | collective-permute-start | bytes 392 | tf_op jit(solution)/shard_map/ppermute | solution.py:18
  410.4 24.3 %collective-permute-start.84 = (f32[1,2,16]{2,1,0:T(2,128)S(1)}, f32[1,2,16]{2,1,0:T(2,128)S(1)}, u32[]{:S(2)}, u32[]{:S(2)}) collective-permute-start(f32[1,2,16]{2,1,0:T(2,128)S(1)} %get-tuple-element.279), channel_id=1, source_target_pairs={{0,16},{1,17},{2,18},{3,19},{4,20},{5,21},{6,22},{7,23},{8,24},{9,... | collective-permute-start | bytes 392 | tf_op jit(solution)/shard_map/ppermute | solution.py:18
  410.4 24.3 %collective-permute-start.85 = (f32[1,2,16]{2,1,0:T(2,128)S(1)}, f32[1,2,16]{2,1,0:T(2,128)S(1)}, u32[]{:S(2)}, u32[]{:S(2)}) collective-permute-start(f32[1,2,16]{2,1,0:T(2,128)S(1)} %get-tuple-element.280), channel_id=1, source_target_pairs={{0,48},{1,49},{2,50},{3,51},{4,52},{5,53},{6,54},{7,55},{8,56},{9,... | collective-permute-start | bytes 392 | tf_op jit(solution)/shard_map/ppermute | solution.py:18
  413.6 21.0 %collective-permute-start.86 = (f32[2,1,16]{2,1,0:T(1,128)S(1)}, f32[2,1,16]{2,1,0:T(1,128)S(1)}, u32[]{:S(2)}, u32[]{:S(2)}) collective-permute-start(f32[2,1,16]{2,1,0:T(1,128)S(1)} %get-tuple-element.281), channel_id=1, source_target_pairs={{0,4},{1,5},{2,6},{3,7},{4,8},{5,9},{6,10},{7,11},{8,12},{9,13},{1... | collective-permute-start | bytes 392 | tf_op jit(solution)/shard_map/ppermute | solution.py:18
  434.9 23.9 %collective-permute-start.90 = (f32[1,2,16]{2,1,0:T(2,128)S(1)}, f32[1,2,16]{2,1,0:T(2,128)S(1)}, u32[]{:S(2)}, u32[]{:S(2)}) collective-permute-start(f32[1,2,16]{2,1,0:T(2,128)S(1)} %get-tuple-element.271), channel_id=1, source_target_pairs={{0,16},{1,17},{2,18},{3,19},{4,20},{5,21},{6,22},{7,23},{8,24},{9,... | collective-permute-start | bytes 392 | tf_op jit(solution)/shard_map/ppermute | solution.py:18
  434.9 23.9 %collective-permute-start.91 = (f32[1,2,16]{2,1,0:T(2,128)S(1)}, f32[1,2,16]{2,1,0:T(2,128)S(1)}, u32[]{:S(2)}, u32[]{:S(2)}) collective-permute-start(f32[1,2,16]{2,1,0:T(2,128)S(1)} %get-tuple-element.272), channel_id=1, source_target_pairs={{0,48},{1,49},{2,50},{3,51},{4,52},{5,53},{6,54},{7,55},{8,56},{9,... | collective-permute-start | bytes 392 | tf_op jit(solution)/shard_map/ppermute | solution.py:18
  (141 other events, 2490.8 us)
where the time goes:
time: 605 us; the launch traced here: 595 us
  waiting for transfers between devices  234 us (39%)
  starting transfers between devices  229 us (38%)
  local copies, waits for them, and re-layouts  90.9 us (15%)
  other arithmetic  36.9 us (6%)
    ppermute x138, waiting for transfers between devices, shifted(): lax.ppermute(shard, axis, [(i, (i + by) % peers) for i in range(peers)])  234 us
    ppermute x138, starting transfers between devices, shifted(): lax.ppermute(shard, axis, [(i, (i + by) % peers) for i in range(peers)])  229 us
  transfers between devices with their start and end apart: 138, of which 41 were waited for; matrix products, arithmetic and copies ran while one was open for 19% of the time, Pallas kernels for 0%

commit v1 on v0

v1 whole, which is shorter than its diff:
```python
import functools

import jax
import jax.numpy as jnp
from jax import lax
from jax.experimental import pallas as pl
from jax.experimental.pallas import tpu as pltpu
from jax.sharding import PartitionSpec as P

N = 64
ROTATE = 21
OMEGA = 0.8
F32 = jnp.float32
HI = lax.Precision.HIGHEST
DIRS = [(a, b, c) for a in (-1, 0, 1) for b in (-1, 0, 1) for c in (-1, 0, 1) if (a, b, c) != (0, 0, 0)]


def offset(d):
    return (16 * d[0] + 4 * d[1] + d[2]) % N


def plan0(narr):
    x_at = {1: 0, -1: 6 * narr}
    y_at = {1: 12 * narr, -1: 20 * narr}
    z_at = {1: 28 * narr, -1: 28 * narr + 2}
    plan, got = {}, 0
    for d in DIRS:
        dx, dy, dz = d
        if dz:
            src, count = z_at[dz] + (1 if dy < 0 else 0), 2 if dy == 0 else 1
        elif dy:
            src, count = y_at[dy] + (6 * narr if dx < 0 else 0), (8 if dx == 0 else 2) * narr
        else:
            src, count = x_at[dx], 6 * narr
        plan[d] = (src, got, count)
        got += count
    return plan, 28 * narr + 4, got


def plan1():
    plan, got = {}, 0
    for d in DIRS:
        dx, dy, dz = d
        if dz:
            src, count = 4, 1
        elif dx:
            src, count = (0 if dx > 0 else 2), 2
        else:
            src, count = 0, 4
        plan[d] = (src, got, count)
        got += count
    return plan, 5, got


PLAN2, SEND2, GOT2 = plan0(2)
PLANV, SENDV, GOTV = plan0(1)
PLAN1, SEND1, GOT1 = plan1()
GATHER = sorted(o for o in range(1, N) if o % 4 != 2)
SLOT = {o: i for i, o in enumerate(GATHER)}
SLOT[0] = len(GATHER)


def rows_of(shape):
    return lax.broadcasted_iota(jnp.int32, shape, len(shape) - 2)


def lanes_of(shape):
    return lax.broadcasted_iota(jnp.int32, shape, len(shape) - 1)


def rot(v, by, axis):
    by %= v.shape[axis]
    return pltpu.roll(v, by, axis) if by else v


def layer_loop(low, high, body, unroll=2):
    def step(x, carry):
        body(x)
        return carry

    lax.fori_loop(low, high, step, 0, unroll=unroll)


def start_to(me, src, dst, send, recv, off):
    pltpu.make_async_remote_copy(
        src_ref=src,
        dst_ref=dst,
        send_sem=send,
        recv_sem=recv,
        device_id={"space": lax.rem(me + (N - off) % N, N)},
        device_id_type=pl.DeviceIdType.MESH,
    ).start()


def send_plan(me, plan, sb, rb, send, recv):
    for d in sorted(plan, key=lambda d: -sum(map(abs, d))):
        src, got, count = plan[d]
        start_to(me, sb.at[pl.ds(src, count)], rb.at[pl.ds(got, count)], send, recv, offset(d))


def wait_got(rb, recv):
    pltpu.make_async_copy(rb, rb, recv).wait()


def wait_sent(rb, send):
    pltpu.make_async_copy(rb, rb, send).wait()


def pack0(own, narr, sb):
    x_at = {1: 0, -1: 6 * narr}
    y_at = {1: 12 * narr, -1: 20 * narr}
    z_at = {1: 28 * narr, -1: 28 * narr + 2}
    low4 = rows_of((8, 128)) < 4
    group = lanes_of((16, 128)) // 4
    zlo = zhi = jnp.zeros((16, 128), F32)
    for a in range(narr):
        for i in range(3):
            for side, x in ((1, i), (-1, 13 + i)):
                v = own(a, x)
                sb[x_at[side] + a * 6 + 2 * i] = v[0:8]
                sb[x_at[side] + a * 6 + 2 * i + 1] = v[8:16]
        for i in range(8):
            v, w = own(a, i), own(a, i + 8)
            sb[y_at[1] + i * narr + a] = jnp.where(low4, v[0:8], rot(w[0:8], 4, 0))
            sb[y_at[-1] + i * narr + a] = jnp.where(low4, rot(w[8:16], 4, 0), v[8:16])
        for x in range(16):
            v, g = own(a, x), 16 * a + x
            zlo = jnp.where(group == g, rot(v, 4 * g, 1), zlo)
            zhi = jnp.where(group == g, rot(v, 4 * g + 4, 1), zhi)
    for side, z in ((1, zlo), (-1, zhi)):
        sb[z_at[side]] = z[0:8]
        sb[z_at[side] + 1] = z[8:16]


def unpack0(a, narr, plan, rb, out):
    low4 = rows_of((8, 128)) < 4

    def at(d):
        return plan[d][1]

    for i in range(3):
        for dx, base in ((1, 20), (-1, 1)):
            first = at((dx, 0, 0)) + a * 6 + 2 * i
            out[base + i, 0:8, 0:128] = rb[first]
            out[base + i, 8:16, 0:128] = rb[first + 1]
    for i in range(8):
        up, lo = rb[at((0, 1, 0)) + i * narr + a], rb[at((0, -1, 0)) + i * narr + a]
        out[4 + i, 16:24, 0:128] = jnp.where(low4, up, lo)
        out[12 + i, 16:24, 0:128] = rot(jnp.where(low4, lo, up), 4, 0)
    for i in range(2):
        up, lo = rb[at((1, 1, 0)) + i * narr + a], rb[at((1, -1, 0)) + i * narr + a]
        out[20 + i, 16:24, 0:128] = jnp.where(low4, up, lo)
        up, lo = rb[at((-1, 1, 0)) + i * narr + a], rb[at((-1, -1, 0)) + i * narr + a]
        out[2 + i, 16:24, 0:128] = rot(jnp.where(low4, lo, up), 4, 0)
    half = lanes_of((24, 128)) < 64
    for dx, layers in ((0, range(4, 20)), (1, range(20, 23)), (-1, range(1, 4))):
        parts = {}
        for dz in (1, -1):
            mid = at((dx, 0, dz))
            tail = jnp.where(low4, rb[at((dx, 1, dz))], rb[at((dx, -1, dz))])
            parts[dz] = jnp.concatenate([rb[mid], rb[mid + 1], tail], axis=0)
        for x in layers:
            g = 16 * a + (x - 4) % 16
            out[x, :, 128:256] = jnp.where(half, rot(parts[1], -4 * g, 1), rot(parts[-1], 124 - 4 * g, 1))


def shifts0(ref, x):
    v = ref[x]
    return v, (
        ref[x - 1],
        ref[x + 1],
        pltpu.roll(v, 1, 0),
        pltpu.roll(v, 23, 0),
        pltpu.roll(v, 1, 1),
        pltpu.roll(v, 255, 1),
    )


def coefs_of(k, near):
    faces = [k + n for n in near]
    total = ((faces[0] + faces[1]) + (faces[2] + faces[3])) + (faces[4] + faces[5])
    inv = OMEGA / total
    return [f * inv for f in faces], 0.5 * total


def change(v, near, gs, c):
    t = [g * (n - v) for g, n in zip(gs, near)]
    return c + (((t[0] + t[1]) + (t[2] + t[3])) + (t[4] + t[5]))


def sweep0(cur, out, g, c, low, high):
    def body(x):
        v, near = shifts0(cur, x)
        out[x] = v + change(v, near, [g[i, x] for i in range(6)], c[x])

    layer_loop(low, high, body)


def own_residual0(cur, g, c, t, x):
    v, near = shifts0(cur, x)
    r = change(v, near, [g[i, x] for i in range(6)], c[x]) * t[x]
    return v, r[0:16, 0:128]


def pack1(w, sb):
    half = lanes_of((8, 128)) < 64
    lane = lanes_of((8, 128))
    for j in range(4):
        sb[j] = jnp.where(half, w[2 * j], w[2 * j + 1])
    z = jnp.zeros((8, 128), F32)
    for x in range(8):
        z = jnp.where(lane // 8 == 2 * x, rot(w[x], 16 * x, 1), z)
        z = jnp.where(lane // 8 == 2 * x + 1, rot(w[x], 16 * x + 8 - 60, 1), z)
    sb[4] = z


def unpack1(w, rb, out):
    half, quarter = lanes_of((8, 128)) < 64, lanes_of((8, 128)) < 96
    low4 = rows_of((8, 128)) < 4

    def block(dx, dy, x):
        if (dx, dy) == (0, 0):
            return w[x]
        first = 2 if dx < 0 else 0
        tile = rb[PLAN1[(dx, dy, 0)][1] + x // 2 - first]
        return rot(tile, 64, 1) if x % 2 else tile

    for dx, layers in ((0, range(8)), (1, range(4)), (-1, range(4, 8))):
        tail = {dz: rb[PLAN1[(dx, 0, dz)][1]] for dz in (1, -1)}
        tail1 = {
            dz: jnp.where(low4, rb[PLAN1[(dx, 1, dz)][1]], rb[PLAN1[(dx, -1, dz)][1]]) for dz in (1, -1)
        }
        for x in layers:
            ends = [jnp.where(quarter, rot(q[1], 64 - 16 * x, 1), rot(q[-1], 116 - 16 * x, 1)) for q in (tail, tail1)]
            out[4 + x + 8 * dx, 0:8] = jnp.where(half, block(dx, 0, x), ends[0])
            rows = jnp.where(low4, block(dx, 1, x), block(dx, -1, x))
            out[4 + x + 8 * dx, 8:16] = jnp.where(half, rows, ends[1])


def shifts1(ref, x):
    v = ref[x]
    return v, (
        ref[x - 1],
        ref[x + 1],
        pltpu.roll(v, 1, 0),
        pltpu.roll(v, 15, 0),
        pltpu.roll(v, 1, 1),
        pltpu.roll(v, 127, 1),
    )


def shifts_round(ref, x, step, lane_step):
    layers, rows = ref.shape[0], ref.shape[1]
    v = ref[x]
    row = rows_of(v.shape)
    below, above = ref[lax.rem(x + layers - step, layers)], ref[lax.rem(x + step, layers)]
    return v, (
        ref[lax.rem(x + layers - 1, layers)],
        ref[lax.rem(x + 1, layers)],
        pltpu.roll(jnp.where(row == rows - 1, below, v), 1, 0),
        pltpu.roll(jnp.where(row == 0, above, v), rows - 1, 0),
        pltpu.roll(v, lane_step, 1),
        pltpu.roll(v, 128 - lane_step, 1),
    )


def pack2(w2, sb):
    group = lanes_of((8, 128)) // 32
    z = w2[0]
    for x in range(1, 4):
        z = jnp.where(group == x, w2[x], z)
    sb[...] = z


def unpack2(rb, out):
    low4 = rows_of((8, 128)) < 4
    group = lanes_of((8, 128)) // 32
    for cx in range(4):
        for t in range(2):
            tiles = {}
            for dz in (-1, 0, 1):
                first = rb[SLOT[(16 * cx + 8 * t + dz) % N]]
                second = rb[SLOT[(16 * cx + 8 * t + 4 + dz) % N]]
                tiles[dz] = jnp.where(low4, first, second)
            for x in range(4):
                z = rot(tiles[0], -32 * x, 1)
                z = jnp.where(group == 1, rot(tiles[1], 32 - 32 * x, 1), z)
                z = jnp.where(group == 3, rot(tiles[-1], 96 - 32 * x, 1), z)
                out[4 * cx + x, 8 * t : 8 * t + 8] = z


def pair_rows(ref, index, count):
    return ref[index, pl.ds(0, count, stride=2), :] + ref[index, pl.ds(1, count, stride=2), :]


def kernel(
    cls_ref, val_ref, cell_ref, rate_ref, guess_ref, p_ref, r_ref,
    fr, vb, kf, g0, t0, c0, u0, sb2, rb2, sbv, rbv,
    pair, w1, k1, b1, v1, q1, g1, t1, c1, sbk1, rbk1, sbb1, rbb1, sbv1, rbv1,
    pair1, w2, k2, b2, v2, q2, g2, t2, c2, sbk2, rbk2, sbb2, rbb2,
    pair2, k3, v3, q3, g3, t3, c3, exp3, exp2, exp1, send, recv,
):
    me = lax.axis_index("space")
    barrier = pltpu.get_barrier_semaphore()
    for o in GATHER:
        pl.semaphore_signal(
            barrier, inc=1, device_id={"space": lax.rem(me + o, N)}, device_id_type=pl.DeviceIdType.MESH
        )

    def lookup(x):
        cls = cls_ref[0, x]
        b0, b1_, b2_ = (cls & 1) == 0, (cls & 2) == 0, (cls & 4) == 0
        pairs = [jnp.where(b0, val_ref[2 * i], val_ref[2 * i + 1]) for i in range(4)]
        quads = [jnp.where(b1_, pairs[0], pairs[1]), jnp.where(b1_, pairs[2], pairs[3])]
        kf[x + 4, 0:16, 0:128] = jnp.where(b2_, quads[0], quads[1])
        fr[x + 4, 0:16, 0:128] = guess_ref[0, x]

    layer_loop(0, 16, lookup)
    pack0(lambda a, x: (fr if a == 0 else kf)[x + 4, 0:16, 0:128], 2, sb2)

    pl.semaphore_wait(barrier, len(GATHER))
    send_plan(me, PLAN2, sb2, rb2, send.at[0], recv.at[0])

    def same(shape, f):
        return f(rows_of(shape), lanes_of(shape)).astype(F32)

    pool0 = same((128, 128), lambda l, c: l // 2 == c % 64)
    pool1 = same((128, 128), lambda l, c: (l // 2 == c % 32) & (l < 64))

    def coarsen0(layer):
        def body(x):
            pair[x] = layer(2 * x) + layer(2 * x + 1)

        layer_loop(0, 8, body, 1)
        sums = jnp.concatenate([pair_rows(pair, x, 8) for x in range(8)], axis=0)
        out = jnp.dot(0.125 * sums, pool0, precision=HI, preferred_element_type=F32)
        for x in range(8):
            w1[x] = out[8 * x : 8 * x + 8]

    def coarsen1(ref, base):
        for x in range(4):
            pair1[x] = ref[base + 2 * x] + ref[base + 2 * x + 1]
        rows = [pair_rows(pair1, x, 4) for x in range(4)]
        sums = jnp.concatenate([q for r in rows for q in (r, r)], axis=0)
        out = jnp.dot(0.125 * sums, pool1, precision=HI, preferred_element_type=F32)
        for x in range(4):
            w2[x] = out[8 * x : 8 * x + 8]

    even = lanes_of((8, 128)) % 2 == 0

    def coarsen2(ref, out):
        for x in range(8):
            pair2[x] = ref[2 * x] + ref[2 * x + 1]
        for x in range(8):
            s = 0.125 * pair_rows(pair2, x, 8)
            out[x] = s + jnp.where(even, pltpu.roll(s, 127, 1), pltpu.roll(s, 1, 1))

    coarsen0(lambda x: kf[x + 4, 0:16, 0:128])
    pack1(w1, sbk1)
    send_plan(me, PLAN1, sbk1, rbk1, send.at[1], recv.at[1])
    q1[0:8, 0:8] = w1[...]
    coarsen1(w1, 0)
    pack2(w2, sbk2)
    for o in GATHER:
        start_to(me, sbk2, rbk2.at[SLOT[o]], send.at[2], recv.at[2], o)

    cell, rate = cell_ref[...], rate_ref[...]
    ix, iy, iz = cell // (64 * 512), cell // 512 % 64, cell % 512
    theirs = (ix // 16 * 4 + iy // 16) * 4 + iz // 128
    place = lax.rem(theirs - lax.rem(me + ROTATE, N) + 2 * N + 21, N)
    dx, dy, dz = place // 16, place // 4 % 4, place % 4
    fx, fy, fz = ix % 16 + 16 * (dx - 1) + 4, iy % 16 + 16 * (dy - 1), iz % 128 + 128 * (dz - 1)
    held = (dx < 3) & (dy < 3) & (dz < 3) & (fy >= -4) & (fy < 20) & (fz >= -4) & (fz < 132)
    fy, fz = jnp.where(fy < 0, fy + 24, fy), jnp.where(fz < 0, fz + 256, fz)
    rate = jnp.where(held, rate, 0.0)
    in_y = jnp.where(rows_of((24, 16)) == fy, rate, 0.0)
    in_z = jnp.where(rows_of((256, 16)) == fz, 1.0, 0.0)
    left = jnp.concatenate([jnp.where(fx == x, in_y, 0.0) for x in range(24)], axis=0)
    c0[...] = lax.dot_general(
        left, in_z, (((1,), (1,)), ((), ())), precision=HI, preferred_element_type=F32
    ).reshape(24, 24, 256)

    wait_got(rb2, recv.at[0])
    unpack0(0, 2, PLAN2, rb2, fr)
    unpack0(1, 2, PLAN2, rb2, kf)

    def coefs0(x):
        k, near = shifts0(kf, x)
        gs, total = coefs_of(k, near)
        for i in range(6):
            g0[i, x] = gs[i]
        t0[x] = (1.0 / OMEGA) * total
        c0[x] = OMEGA * c0[x] / total

    layer_loop(2, 22, coefs0, 1)
    sweep0(fr, vb, g0, c0, 2, 22)
    sweep0(vb, u0, g0, c0, 3, 21)
    coarsen0(lambda x: own_residual0(u0, g0, c0, t0, x + 4)[1])
    pack1(w1, sbb1)
    send_plan(me, PLAN1, sbb1, rbb1, send.at[3], recv.at[3])
    pack0(lambda a, x: u0[x + 4, 0:16, 0:128], 1, sbv)
    send_plan(me, PLANV, sbv, rbv, send.at[4], recv.at[4])

    wait_got(rbk1, recv.at[1])
    unpack1(q1, rbk1, k1)

    def coefs1(x):
        k, near = shifts1(k1, x)
        gs, total = coefs_of(k, near)
        for i in range(6):
            g1[i, x] = gs[i]
        t1[x] = 0.25 * total

    layer_loop(1, 15, coefs1, 1)
    rbk2[SLOT[0]] = sbk2[...]
    wait_got(rbk2.at[pl.ds(0, len(GATHER))], recv.at[2])
    unpack2(rbk2, k2)
    outside = lanes_of((16, 128)) // 32 == 2

    def fill2(x):
        k2[x] = jnp.where(outside, 1.0, k2[x])

    layer_loop(0, 16, fill2)

    def coefs2(x):
        k, near = shifts_round(k2, x, 4, 1)
        gs, total = coefs_of(k, near)
        for i in range(6):
            g2[i, x] = gs[i]
        t2[x] = 0.0625 * total

    layer_loop(0, 16, coefs2, 1)
    coarsen2(k2, k3)

    def coefs3(x):
        k, near = shifts_round(k3, x, 2, 2)
        gs, total = coefs_of(k, near)
        for i in range(6):
            g3[i, x] = gs[i]
        t3[x] = 0.015625 * total

    layer_loop(0, 8, coefs3, 1)

    wait_got(rbb1, recv.at[3])
    unpack1(w1, rbb1, b1)

    def first1(x):
        c1[x] = OMEGA * b1[x] / t1[x]

    layer_loop(1, 15, first1)

    def sweep1(cur, out, low, high):
        def body(x):
            v, near = shifts1(cur, x)
            out[x] = v + change(v, near, [g1[i, x] for i in range(6)], c1[x])

        layer_loop(low, high, body)

    sweep1(c1, v1, 3, 13)

    def down1(x):
        v, near = shifts1(v1, x)
        r = change(v, near, [g1[i, x] for i in range(6)], c1[x]) * t1[x]
        q1[x] = (1.0 / OMEGA) * r[0:8]

    layer_loop(4, 12, down1)
    coarsen1(q1, 4)
    pack2(w2, sbb2)
    for o in GATHER:
        start_to(me, sbb2, rbb2.at[SLOT[o]], send.at[6], recv.at[6], o)
    half = lanes_of((8, 128)) < 64
    for x in range(8):
        v = v1[x + 4, 0:8]
        w1[x] = jnp.where(half, v, pltpu.roll(v, 64, 1))
    pack1(w1, sbv1)
    send_plan(me, PLAN1, sbv1, rbv1, send.at[5], recv.at[5])

    wait_sent(rb2, send.at[0])
    wait_sent(rbk1, send.at[1])
    wait_sent(rbk2.at[pl.ds(0, len(GATHER))], send.at[2])
    wait_sent(rbb1, send.at[3])
    wait_sent(rbv, send.at[4])
    wait_got(rbv, recv.at[4])
    unpack0(0, 1, PLANV, rbv, u0)
    wait_got(rbv1, recv.at[5])
    unpack1(w1, rbv1, v1)
    wait_sent(rbv1, send.at[5])

    rbb2[SLOT[0]] = sbb2[...]
    wait_got(rbb2.at[pl.ds(0, len(GATHER))], recv.at[6])
    unpack2(rbb2, b2)

    def first2(x):
        c2[x] = OMEGA * jnp.where(outside, 0.0, b2[x]) / t2[x]

    layer_loop(0, 16, first2)

    def sweep2(cur, out):
        def body(x):
            v, near = shifts_round(cur, x, 4, 1)
            out[x] = v + change(v, near, [g2[i, x] for i in range(6)], c2[x])

        layer_loop(0, 16, body)

    sweep2(c2, v2)

    def down2(x):
        v, near = shifts_round(v2, x, 4, 1)
        r = change(v, near, [g2[i, x] for i in range(6)], c2[x]) * t2[x]
        q2[x] = (1.0 / OMEGA) * r

    layer_loop(0, 16, down2)
    coarsen2(q2, c3)

    def first3(x):
        c3[x] = OMEGA * c3[x] / t3[x]

    layer_loop(0, 8, first3)

    def sweep3(cur, out):
        def body(x):
            v, near = shifts_round(cur, x, 2, 2)
            out[x] = v + change(v, near, [g3[i, x] for i in range(6)], c3[x])

        layer_loop(0, 8, body)

    sweep3(c3, v3)
    sweep3(v3, q3)
    sweep3(q3, v3)
    sweep3(v3, q3)
    sweep3(q3, v3)

    def up2(x):
        e = v3[x]
        exp3[x, pl.ds(0, 8, stride=2), :] = e
        exp3[x, pl.ds(1, 8, stride=2), :] = e
        q2[2 * x] = v2[2 * x] + exp3[x]
        q2[2 * x + 1] = v2[2 * x + 1] + exp3[x]

    layer_loop(0, 8, up2, 1)
    sweep2(q2, v2)
    sweep2(v2, q2)

    spread2 = same((128, 128), lambda c, f: c == jnp.where(f < 96, f // 2, 64 + f // 2))
    row = rows_of((8, 128))
    order = [14, 15, 0, 1, 2, 3, 4, 5]
    rows = [jnp.where(row < 6, q2[x, 0:8], q2[(x - 4) % 16, 8:16]) for x in order]
    out = jnp.dot(jnp.concatenate(rows, axis=0), spread2, precision=HI, preferred_element_type=F32)
    for i in range(8):
        e = out[8 * i : 8 * i + 8]
        exp2[i, pl.ds(0, 8, stride=2), :] = e
        exp2[i, pl.ds(1, 8, stride=2), :] = e
    for x in range(16):
        b1[x] = v1[x] + exp2[x // 2]
    sweep1(b1, v1, 1, 15)
    sweep1(v1, b1, 2, 14)

    def spread(c, f):
        return c == jnp.where(f < 192, f // 2, f // 2)

    spread1 = same((128, 256), spread)
    inside = (lanes_of((16, 128)) < 66) | (lanes_of((16, 128)) >= 126)
    rows = [jnp.where(inside, b1[x], 0.0) for x in range(2, 14)]
    out = jnp.dot(jnp.concatenate(rows, axis=0), spread1, precision=HI, preferred_element_type=F32)
    low4 = rows_of((8, 256)) < 4
    for i in range(12):
        for h in range(2):
            e = out[16 * i : 16 * i + 16, 128 * h : 128 * h + 128]
            exp1[i, h, pl.ds(0, 16, stride=2), :] = e
            exp1[i, h, pl.ds(1, 16, stride=2), :] = e
    low4 = rows_of((8, 128)) < 4
    for i in range(12):
        for h in range(2):
            tail = jnp.where(low4, exp1[i, h, 16:24], exp1[i, h, 24:32])
            for x in (2 * i, 2 * i + 1):
                if 1 <= x < 23:
                    at = pl.ds(128 * h, 128)
                    vb[x, 0:16, at] = u0[x, 0:16, at] + exp1[i, h, 0:16]
                    vb[x, 16:24, at] = u0[x, 16:24, at] + tail
    sweep0(vb, u0, g0, c0, 2, 22)
    sweep0(u0, vb, g0, c0, 3, 21)

    def finish(x):
        v, r = own_residual0(vb, g0, c0, t0, x + 4)
        p_ref[0, x] = v[0:16, 0:128]
        r_ref[0, x] = r

    layer_loop(0, 16, finish)
    wait_sent(rbb2.at[pl.ds(0, len(GATHER))], send.at[6])


def shards(perm_class, class_values, well_cells, well_rates, guess):
    wells = well_cells.shape[0]

    def f(*shape):
        return pltpu.VMEM(shape, F32)

    t = (8, 128)
    l0, l1, l2, l3 = (24, 24, 256), (16, 16, 128), (16, 16, 128), (8, 8, 128)
    vmem = pl.BlockSpec(memory_space=pltpu.VMEM)
    block = jax.ShapeDtypeStruct(guess.shape, F32)
    return pl.pallas_call(
        kernel,
        out_shape=(block, block),
        in_specs=[vmem, pl.BlockSpec(memory_space=pltpu.SMEM), vmem, vmem, vmem],
        out_specs=(vmem, vmem),
        scratch_shapes=[
            f(*l0), f(*l0), f(*l0), f(6, *l0), f(*l0), f(*l0), f(*l0),
            f(SEND2, *t), f(GOT2, *t), f(SENDV, *t), f(GOTV, *t),
            f(8, 16, 128), f(8, *t), f(*l1), f(*l1), f(*l1), f(16, *t), f(6, *l1), f(*l1), f(*l1),
            f(SEND1, *t), f(GOT1, *t), f(SEND1, *t), f(GOT1, *t), f(SEND1, *t), f(GOT1, *t),
            f(4, *t), f(4, *t), f(*l2), f(*l2), f(*l2), f(*l2), f(6, *l2), f(*l2), f(*l2),
            f(*t), f(len(GATHER) + 1, *t), f(*t), f(len(GATHER) + 1, *t),
            f(8, 16, 128), f(*l3), f(*l3), f(*l3), f(6, *l3), f(*l3), f(*l3),
            f(8, 16, 128), f(8, 16, 128), f(12, 2, 32, 128),
            pltpu.SemaphoreType.DMA((7,)), pltpu.SemaphoreType.DMA((7,)),
        ],
        compiler_params=pltpu.CompilerParams(
            collective_id=0, has_side_effects=True, vmem_limit_bytes=40 * 1024 * 1024
        ),
    )(perm_class, class_values, well_cells.reshape(1, wells), well_rates.reshape(1, wells), guess)


def solution(mesh):
    whole = P(("real", "space"), None, None, None)
    return jax.shard_map(
        shards,
        mesh=mesh,
        in_specs=(P("space", None, None, None), P(), P("real"), P("real"), whole),
        out_specs=(whole, whole),
        check_vma=False,
    )
```

time: 605 us -> 59.2 us (0.10); the launches traced: 595 us -> 59.1 us
  waiting for transfers between devices: 234 us -> 0 us
  starting transfers between devices: 229 us -> 0 us
  local copies, waits for them, and re-layouts: 90.9 us -> 3.78 us
  Pallas kernels: 0 us -> 54.6 us
  other arithmetic: 36.9 us -> 0 us
    ppermute x138 -> x0, waiting for transfers between devices: 234 us -> none  [shifted(): lax.ppermute(shard, axis, [(i, (i + by) % peers) for i in range(peers)])]
    ppermute x138 -> x0, starting transfers between devices: 229 us -> none  [shifted(): lax.ppermute(shard, axis, [(i, (i + by) % peers) for i in range(peers)])]
    pallas_call x0 -> x1, Pallas kernels: none -> 54.6 us  [shards(): pl.pallas_call(kernel, out_shape=(block, block), in_specs=[vmem, pl.Block...]
    concatenate x54 -> x0, local copies, waits for them, and re-layouts: 37.3 us -> none  [the longest x9 6.96 us: exchange_faces(): jnp.concatenate([values[:, 1:], upper_y], axis=1)]
    slice x126 -> x0, local copies, waits for them, and re-layouts: 24.6 us -> none  [the longest x13 3.53 us: exchange_faces(): upper_z = shifted(values[:, :, :1], 'space', -1)]
    add x19 -> x0, other arithmetic: 16.6 us -> none  [the longest x1 5.93 us: shards(): permeab = permeab + jnp.where(classes == number, class_values[number], 0.0)]
    reduce_sum x6 -> x0, other arithmetic: 11 us -> none  [coarsen(): values.reshape(size_x // 2, 2, size_y // 2, 2, size_z // 2, 2)]
    reshape x7 -> x0, local copies, waits for them, and re-layouts: 10.9 us -> none  [the longest x1 9.76 us: coarsen(): values.reshape(size_x // 2, 2, size_y // 2, 2, size_z // 2, 2)]
  transfers between devices with their start and end apart: 138 -> 0, of which waited for: 41 -> 0; matrix products, arithmetic and copies ran while one was open for 19% -> 0% of each run, Pallas kernels for 0% -> 0%
where the time goes in v1:
time: 59.2 us; the launch traced here: 59.1 us
  Pallas kernels  54.6 us (92%)
  local copies, waits for them, and re-layouts  3.78 us (6%)
  between operations  0.67 us (1%)
    pallas_call x1, Pallas kernels, shards(): pl.pallas_call(kernel, out_shape=(block, block), in_specs=[vmem, pl.Block...  54.6 us
    unnamed x12, local copies, waits for them, and re-layouts  3.78 us

profile of v1, /device:TPU:2, one launch (start us, length us, event | category | flops | bytes accessed | tf_op | source)
XLA Modules:
  0.0 59.1 jit_solution(1121362658057625077)
XLA Ops:
  0.6 0.0 copy-start.2
  0.6 0.0 copy-start.3
  0.7 0.0 copy-start.4
  0.7 0.6 %copy-done.2 = f32[8]{0:T(128)S(1)} copy-done((f32[8]{0:T(128)S(1)}, f32[8]{0:T(128)}, u32[]{:S(2)}) %copy-start.2) | copy-done | bytes 56
  1.3 0.0 copy-done.3
  1.3 0.0 copy-done.4
  1.3 0.0 copy-start
  1.3 0.9 %copy-done = s32[1,16,16,128]{3,2,1,0:T(8,128)S(1)} copy-done((s32[1,16,16,128]{3,2,1,0:T(8,128)S(1)}, s32[1,16,16,128]{3,2,1,0:T(8,128)}, u32[]{:S(2)}) %copy-start) | copy-done | bytes 131096
  2.2 0.0 copy-start.1
  2.2 0.9 %copy-done.1 = f32[1,16,16,128]{3,2,1,0:T(8,128)S(1)} copy-done((f32[1,16,16,128]{3,2,1,0:T(8,128)S(1)}, f32[1,16,16,128]{3,2,1,0:T(8,128)}, u32[]{:S(2)}) %copy-start.1) | copy-done | bytes 131096
  3.1 54.6 %shard_map.68 = (f32[1,16,16,128]{3,2,1,0:T(8,128)S(1)}, f32[1,16,16,128]{3,2,1,0:T(8,128)S(1)}) custom-call(s32[1,16,16,128]{3,2,1,0:T(8,128)S(1)} %copy-done, f32[8]{0:T(128)S(1)} %copy-done.2, s32[1,16]{1,0:T(1,128)S(1)} %bitcast.2, f32[1,16]{1,0:T(1,128)S(1)} %bitcast.3, f32[1,16,16,128]{3,2,1,0:T(8,128)S(1)} %copy-done.1), custom_call_target="tpu_custom_call" | custom-call | tf_op jit(solution)/shard_map/pallas_call | solution.py:602
  57.8 0.7 %copy.9 = f32[1,16,16,128]{3,2,1,0:T(8,128)} copy(f32[1,16,16,128]{3,2,1,0:T(8,128)S(1)} %get-tuple-element.4) | data formatting | bytes 262144
  58.4 0.7 %copy.10 = f32[1,16,16,128]{3,2,1,0:T(8,128)} copy(f32[1,16,16,128]{3,2,1,0:T(8,128)S(1)} %get-tuple-element.5) | data formatting | bytes 262144
Async XLA Ops:
  0.6 0.7 %copy-start.2 = (f32[8]{0:T(128)S(1)}, f32[8]{0:T(128)}, u32[]{:S(2)}) copy-start(f32[8]{0:T(128)} %val_ref.1) | copy-start | bytes 100
  0.6 0.7 %copy-start.3 = (s32[16]{0:T(128)S(1)}, s32[16]{0:T(128)}, u32[]{:S(2)}) copy-start(s32[16]{0:T(128)} %param.7) | copy-start | bytes 196
  0.7 0.7 %copy-start.4 = (f32[16]{0:T(128)S(1)}, f32[16]{0:T(128)}, u32[]{:S(2)}) copy-start(f32[16]{0:T(128)} %param.8) | copy-start | bytes 196
  1.3 0.9 %copy-start = (s32[1,16,16,128]{3,2,1,0:T(8,128)S(1)}, s32[1,16,16,128]{3,2,1,0:T(8,128)}, u32[]{:S(2)}) copy-start(s32[1,16,16,128]{3,2,1,0:T(8,128)} %cls_ref.1) | copy-start | bytes 393220
  2.2 0.9 %copy-start.1 = (f32[1,16,16,128]{3,2,1,0:T(8,128)S(1)}, f32[1,16,16,128]{3,2,1,0:T(8,128)}, u32[]{:S(2)}) copy-start(f32[1,16,16,128]{3,2,1,0:T(8,128)} %guess_ref.1) | copy-start | bytes 393220

commit v2 on v1

--- a/solution.py
+++ b/solution.py
@@ -73,12 +73,12 @@
     return pltpu.roll(v, by, axis) if by else v
 
 
-def layer_loop(low, high, body, unroll=2):
+def layer_loop(low, high, body, unroll=None):
     def step(x, carry):
         body(x)
         return carry
 
-    lax.fori_loop(low, high, step, 0, unroll=unroll)
+    lax.fori_loop(low, high, step, 0, unroll=unroll or high - low)
 
 
 def start_to(me, src, dst, send, recv, off):
@@ -331,7 +331,7 @@
         def body(x):
             pair[x] = layer(2 * x) + layer(2 * x + 1)
 
-        layer_loop(0, 8, body, 1)
+        layer_loop(0, 8, body)
         sums = jnp.concatenate([pair_rows(pair, x, 8) for x in range(8)], axis=0)
         out = jnp.dot(0.125 * sums, pool0, precision=HI, preferred_element_type=F32)
         for x in range(8):
@@ -392,7 +392,7 @@
         t0[x] = (1.0 / OMEGA) * total
         c0[x] = OMEGA * c0[x] / total
 
-    layer_loop(2, 22, coefs0, 1)
+    layer_loop(2, 22, coefs0)
     sweep0(fr, vb, g0, c0, 2, 22)
     sweep0(vb, u0, g0, c0, 3, 21)
     coarsen0(lambda x: own_residual0(u0, g0, c0, t0, x + 4)[1])
@@ -411,7 +411,7 @@
             g1[i, x] = gs[i]
         t1[x] = 0.25 * total
 
-    layer_loop(1, 15, coefs1, 1)
+    layer_loop(1, 15, coefs1)
     rbk2[SLOT[0]] = sbk2[...]
     wait_got(rbk2.at[pl.ds(0, len(GATHER))], recv.at[2])
     unpack2(rbk2, k2)
@@ -429,7 +429,7 @@
             g2[i, x] = gs[i]
         t2[x] = 0.0625 * total
 
-    layer_loop(0, 16, coefs2, 1)
+    layer_loop(0, 16, coefs2)
     coarsen2(k2, k3)
 
     def coefs3(x):
@@ -439,7 +439,7 @@
             g3[i, x] = gs[i]
         t3[x] = 0.015625 * total
 
-    layer_loop(0, 8, coefs3, 1)
+    layer_loop(0, 8, coefs3)
 
     wait_got(rbb1, recv.at[3])
     unpack1(w1, rbb1, b1)
@@ -537,7 +537,7 @@
         q2[2 * x] = v2[2 * x] + exp3[x]
         q2[2 * x + 1] = v2[2 * x + 1] + exp3[x]
 
-    layer_loop(0, 8, up2, 1)
+    layer_loop(0, 8, up2)
     sweep2(q2, v2)
     sweep2(v2, q2)
 

time: 59.2 us -> 50.3 us (0.85)
  Pallas kernels: 54.6 us -> 45.7 us
    pallas_call x1, Pallas kernels: 54.6 us -> 45.7 us  [shards(): pl.pallas_call(kernel, out_shape=(block, block), in_specs=[vmem, pl.Block...]
where the time goes in v2:
time: 50.3 us; the launch traced here: 50.1 us
  Pallas kernels  45.7 us (91%)
  local copies, waits for them, and re-layouts  3.78 us (8%)
  between operations  0.67 us (1%)
    pallas_call x1, Pallas kernels, shards(): pl.pallas_call(kernel, out_shape=(block, block), in_specs=[vmem, pl.Block...  45.7 us
    unnamed x12, local copies, waits for them, and re-layouts  3.78 us

profile of v2, /device:TPU:2, one launch (start us, length us, event | category | flops | bytes accessed | tf_op | source)
XLA Modules:
  0.0 50.1 jit_solution(4091916153677602921)
XLA Ops:
  0.6 0.0 copy-start.2
  0.6 0.0 copy-start.3
  0.7 0.0 copy-start.4
  0.7 0.6 %copy-done.2 = f32[8]{0:T(128)S(1)} copy-done((f32[8]{0:T(128)S(1)}, f32[8]{0:T(128)}, u32[]{:S(2)}) %copy-start.2) | copy-done | bytes 56
  1.3 0.0 copy-done.3
  1.3 0.0 copy-done.4
  1.3 0.0 copy-start
  1.3 0.9 %copy-done = s32[1,16,16,128]{3,2,1,0:T(8,128)S(1)} copy-done((s32[1,16,16,128]{3,2,1,0:T(8,128)S(1)}, s32[1,16,16,128]{3,2,1,0:T(8,128)}, u32[]{:S(2)}) %copy-start) | copy-done | bytes 131096
  2.2 0.0 copy-start.1
  2.2 0.9 %copy-done.1 = f32[1,16,16,128]{3,2,1,0:T(8,128)S(1)} copy-done((f32[1,16,16,128]{3,2,1,0:T(8,128)S(1)}, f32[1,16,16,128]{3,2,1,0:T(8,128)}, u32[]{:S(2)}) %copy-start.1) | copy-done | bytes 131096
  3.1 45.7 %shard_map.68 = (f32[1,16,16,128]{3,2,1,0:T(8,128)S(1)}, f32[1,16,16,128]{3,2,1,0:T(8,128)S(1)}) custom-call(s32[1,16,16,128]{3,2,1,0:T(8,128)S(1)} %copy-done, f32[8]{0:T(128)S(1)} %copy-done.2, s32[1,16]{1,0:T(1,128)S(1)} %bitcast.2, f32[1,16]{1,0:T(1,128)S(1)} %bitcast.3, f32[1,16,16,128]{3,2,1,0:T(8,128)S(1)} %copy-done.1), custom_call_target="tpu_custom_call" | custom-call | tf_op jit(solution)/shard_map/pallas_call | solution.py:602
  48.8 0.7 %copy.9 = f32[1,16,16,128]{3,2,1,0:T(8,128)} copy(f32[1,16,16,128]{3,2,1,0:T(8,128)S(1)} %get-tuple-element.4) | data formatting | bytes 262144
  49.5 0.7 %copy.10 = f32[1,16,16,128]{3,2,1,0:T(8,128)} copy(f32[1,16,16,128]{3,2,1,0:T(8,128)S(1)} %get-tuple-element.5) | data formatting | bytes 262144
Async XLA Ops:
  0.6 0.7 %copy-start.2 = (f32[8]{0:T(128)S(1)}, f32[8]{0:T(128)}, u32[]{:S(2)}) copy-start(f32[8]{0:T(128)} %val_ref.1) | copy-start | bytes 100
  0.6 0.7 %copy-start.3 = (s32[16]{0:T(128)S(1)}, s32[16]{0:T(128)}, u32[]{:S(2)}) copy-start(s32[16]{0:T(128)} %param.7) | copy-start | bytes 196
  0.7 0.7 %copy-start.4 = (f32[16]{0:T(128)S(1)}, f32[16]{0:T(128)}, u32[]{:S(2)}) copy-start(f32[16]{0:T(128)} %param.8) | copy-start | bytes 196
  1.3 0.9 %copy-start = (s32[1,16,16,128]{3,2,1,0:T(8,128)S(1)}, s32[1,16,16,128]{3,2,1,0:T(8,128)}, u32[]{:S(2)}) copy-start(s32[1,16,16,128]{3,2,1,0:T(8,128)} %cls_ref.1) | copy-start | bytes 393220
  2.2 0.9 %copy-start.1 = (f32[1,16,16,128]{3,2,1,0:T(8,128)S(1)}, f32[1,16,16,128]{3,2,1,0:T(8,128)}, u32[]{:S(2)}) copy-start(f32[1,16,16,128]{3,2,1,0:T(8,128)} %guess_ref.1) | copy-start | bytes 393220

commit v3 on v2

--- a/solution.py
+++ b/solution.py
@@ -19,43 +19,62 @@
     return (16 * d[0] + 4 * d[1] + d[2]) % N
 
 
-def plan0(narr):
+def hops(off):
+    total = 0
+    for row in range(N):
+        to = (row + off) % N
+        y, z = abs(row // 16 - to // 16), abs(row // 2 % 8 - to // 2 % 8)
+        total += min(y, 4 - y) + min(z, 8 - z) + 2 * abs(row % 2 - to % 2)
+    return total
+
+
+def sent0(narr):
     x_at = {1: 0, -1: 6 * narr}
     y_at = {1: 12 * narr, -1: 20 * narr}
-    z_at = {1: 28 * narr, -1: 28 * narr + 2}
+    e_at = {d: 28 * narr + i for i, d in enumerate([(1, 1), (1, -1), (-1, 1), (-1, -1)])}
+    z_at = {1: 28 * narr + 4, -1: 28 * narr + 6}
+    return x_at, y_at, e_at, z_at, 28 * narr + 8
+
+
+def plan0(narr):
+    x_at, y_at, e_at, z_at, length = sent0(narr)
     plan, got = {}, 0
     for d in DIRS:
         dx, dy, dz = d
         if dz:
             src, count = z_at[dz] + (1 if dy < 0 else 0), 2 if dy == 0 else 1
+        elif dx and dy:
+            src, count = e_at[(dx, dy)], 1
         elif dy:
-            src, count = y_at[dy] + (6 * narr if dx < 0 else 0), (8 if dx == 0 else 2) * narr
+            src, count = y_at[dy], 8 * narr
         else:
             src, count = x_at[dx], 6 * narr
         plan[d] = (src, got, count)
         got += count
-    return plan, 28 * narr + 4, got
-
-
-def plan1():
+    return plan, length, got
+
+
+def plan1(narr):
     plan, got = {}, 0
     for d in DIRS:
         dx, dy, dz = d
         if dz:
-            src, count = 4, 1
-        elif dx:
-            src, count = (0 if dx > 0 else 2), 2
+            src, count = 8 * narr, 1
+        elif dy:
+            src = (4 if dy > 0 else 6) * narr + (narr if dx < 0 else 0)
+            count = narr if dx else 2 * narr
         else:
-            src, count = 0, 4
+            src, count = (0 if dx > 0 else 2 * narr), 2 * narr
         plan[d] = (src, got, count)
         got += count
-    return plan, 5, got
+    return plan, 8 * narr + 1, got
 
 
 PLAN2, SEND2, GOT2 = plan0(2)
 PLANV, SENDV, GOTV = plan0(1)
-PLAN1, SEND1, GOT1 = plan1()
-GATHER = sorted(o for o in range(1, N) if o % 4 != 2)
+PLANS1 = {n: plan1(n) for n in (1, 2)}
+NEAR = sorted((offset(d) for d in DIRS), key=lambda o: (-hops(o), o))
+GATHER = sorted((o for o in range(1, N) if o % 4 != 2), key=lambda o: (-hops(o), o))
 SLOT = {o: i for i, o in enumerate(GATHER)}
 SLOT[0] = len(GATHER)
 
@@ -93,7 +112,7 @@
 
 
 def send_plan(me, plan, sb, rb, send, recv):
-    for d in sorted(plan, key=lambda d: -sum(map(abs, d))):
+    for d in sorted(plan, key=lambda d: -hops(offset(d))):
         src, got, count = plan[d]
         start_to(me, sb.at[pl.ds(src, count)], rb.at[pl.ds(got, count)], send, recv, offset(d))
 
@@ -107,10 +126,9 @@
 
 
 def pack0(own, narr, sb):
-    x_at = {1: 0, -1: 6 * narr}
-    y_at = {1: 12 * narr, -1: 20 * narr}
-    z_at = {1: 28 * narr, -1: 28 * narr + 2}
+    x_at, y_at, e_at, z_at, _ = sent0(narr)
     low4 = rows_of((8, 128)) < 4
+    two = rows_of((8, 128)) // 2
     group = lanes_of((16, 128)) // 4
     zlo = zhi = jnp.zeros((16, 128), F32)
     for a in range(narr):
@@ -123,6 +141,15 @@
             v, w = own(a, i), own(a, i + 8)
             sb[y_at[1] + i * narr + a] = jnp.where(low4, v[0:8], rot(w[0:8], 4, 0))
             sb[y_at[-1] + i * narr + a] = jnp.where(low4, rot(w[8:16], 4, 0), v[8:16])
+    for (dx, dy), at in e_at.items():
+        z = jnp.zeros((8, 128), F32)
+        for a in range(narr):
+            for i in range(2):
+                v = own(a, i if dx > 0 else 14 + i)
+                v = v[0:8] if dy > 0 else v[8:16]
+                z = jnp.where(two == 2 * a + i, rot(v, 4 * a + 2 * i - (0 if dy > 0 else 6), 0), z)
+        sb[at] = z
+    for a in range(narr):
         for x in range(16):
             v, g = own(a, x), 16 * a + x
             zlo = jnp.where(group == g, rot(v, 4 * g, 1), zlo)
@@ -147,11 +174,11 @@
         up, lo = rb[at((0, 1, 0)) + i * narr + a], rb[at((0, -1, 0)) + i * narr + a]
         out[4 + i, 16:24, 0:128] = jnp.where(low4, up, lo)
         out[12 + i, 16:24, 0:128] = rot(jnp.where(low4, lo, up), 4, 0)
-    for i in range(2):
-        up, lo = rb[at((1, 1, 0)) + i * narr + a], rb[at((1, -1, 0)) + i * narr + a]
-        out[20 + i, 16:24, 0:128] = jnp.where(low4, up, lo)
-        up, lo = rb[at((-1, 1, 0)) + i * narr + a], rb[at((-1, -1, 0)) + i * narr + a]
-        out[2 + i, 16:24, 0:128] = rot(jnp.where(low4, lo, up), 4, 0)
+    for dx, base in ((1, 20), (-1, 2)):
+        for i in range(2):
+            up = rot(rb[at((dx, 1, 0))], -(4 * a + 2 * i), 0)
+            lo = rot(rb[at((dx, -1, 0))], 6 - (4 * a + 2 * i), 0)
+            out[base + i, 16:24, 0:128] = jnp.where(low4, up, lo)
     half = lanes_of((24, 128)) < 64
     for dx, layers in ((0, range(4, 20)), (1, range(20, 23)), (-1, range(1, 4))):
         parts = {}
@@ -202,39 +229,54 @@
     return v, r[0:16, 0:128]
 
 
-def pack1(w, sb):
-    half = lanes_of((8, 128)) < 64
-    lane = lanes_of((8, 128))
-    for j in range(4):
-        sb[j] = jnp.where(half, w[2 * j], w[2 * j + 1])
+def pack1(ws, sb):
+    narr = len(ws)
+    half, low4 = lanes_of((8, 128)) < 64, rows_of((8, 128)) < 4
+    group = lanes_of((8, 128)) // 4
     z = jnp.zeros((8, 128), F32)
-    for x in range(8):
-        z = jnp.where(lane // 8 == 2 * x, rot(w[x], 16 * x, 1), z)
-        z = jnp.where(lane // 8 == 2 * x + 1, rot(w[x], 16 * x + 8 - 60, 1), z)
-    sb[4] = z
-
-
-def unpack1(w, rb, out):
+    for a, w in enumerate(ws):
+        for j in range(4):
+            sb[j * narr + a] = jnp.where(half, w[2 * j], w[2 * j + 1])
+        for j in range(2):
+            p, q, r, t = (w[4 * j + i] for i in range(4))
+            here, there = jnp.where(half, p, r), rot(jnp.where(half, q, t), 4, 0)
+            sb[(4 + j) * narr + a] = jnp.where(low4, here, there)
+            sb[(6 + j) * narr + a] = jnp.where(low4, there, here)
+        for x in range(8):
+            g = 16 * a + x
+            z = jnp.where(group == g, rot(w[x], 4 * g, 1), z)
+            z = jnp.where(group == g + 8, rot(w[x], 4 * (g + 8) - 60, 1), z)
+    sb[8 * narr] = z
+
+
+def unpack1(a, narr, w, rb, out):
     half, quarter = lanes_of((8, 128)) < 64, lanes_of((8, 128)) < 96
     low4 = rows_of((8, 128)) < 4
-
-    def block(dx, dy, x):
-        if (dx, dy) == (0, 0):
+    plan = PLANS1[narr][0]
+
+    def at(d, j=0):
+        return rb[plan[d][1] + j * narr + a]
+
+    def layer(dx, x):
+        if dx == 0:
             return w[x]
-        first = 2 if dx < 0 else 0
-        tile = rb[PLAN1[(dx, dy, 0)][1] + x // 2 - first]
+        tile = at((dx, 0, 0), x // 2 - (2 if dx < 0 else 0))
         return rot(tile, 64, 1) if x % 2 else tile
 
+    def rows(dx, x):
+        j = x // 4 if dx == 0 else 0
+        up, lo = at((dx, 1, 0), j), at((dx, -1, 0), j)
+        tile = rot(jnp.where(low4, lo, up), 4, 0) if x % 2 else jnp.where(low4, up, lo)
+        return rot(tile, 64, 1) if x % 4 > 1 else tile
+
     for dx, layers in ((0, range(8)), (1, range(4)), (-1, range(4, 8))):
-        tail = {dz: rb[PLAN1[(dx, 0, dz)][1]] for dz in (1, -1)}
-        tail1 = {
-            dz: jnp.where(low4, rb[PLAN1[(dx, 1, dz)][1]], rb[PLAN1[(dx, -1, dz)][1]]) for dz in (1, -1)
-        }
+        tail = {dz: rb[plan[(dx, 0, dz)][1]] for dz in (1, -1)}
+        tail1 = {dz: jnp.where(low4, rb[plan[(dx, 1, dz)][1]], rb[plan[(dx, -1, dz)][1]]) for dz in (1, -1)}
         for x in layers:
-            ends = [jnp.where(quarter, rot(q[1], 64 - 16 * x, 1), rot(q[-1], 116 - 16 * x, 1)) for q in (tail, tail1)]
-            out[4 + x + 8 * dx, 0:8] = jnp.where(half, block(dx, 0, x), ends[0])
-            rows = jnp.where(low4, block(dx, 1, x), block(dx, -1, x))
-            out[4 + x + 8 * dx, 8:16] = jnp.where(half, rows, ends[1])
+            g = 16 * a + x
+            ends = [jnp.where(quarter, rot(q[1], 64 - 4 * g, 1), rot(q[-1], 124 - 4 * (g + 8), 1)) for q in (tail, tail1)]
+            out[4 + x + 8 * dx, 0:8] = jnp.where(half, layer(dx, x), ends[0])
+            out[4 + x + 8 * dx, 8:16] = jnp.where(half, rows(dx, x), ends[1])
 
 
 def shifts1(ref, x):
@@ -269,11 +311,10 @@
     z = w2[0]
     for x in range(1, 4):
         z = jnp.where(group == x, w2[x], z)
-    sb[...] = z
+    sb[...] = z[0:4]
 
 
 def unpack2(rb, out):
-    low4 = rows_of((8, 128)) < 4
     group = lanes_of((8, 128)) // 32
     for cx in range(4):
         for t in range(2):
@@ -281,7 +322,7 @@
             for dz in (-1, 0, 1):
                 first = rb[SLOT[(16 * cx + 8 * t + dz) % N]]
                 second = rb[SLOT[(16 * cx + 8 * t + 4 + dz) % N]]
-                tiles[dz] = jnp.where(low4, first, second)
+                tiles[dz] = jnp.concatenate([first, second], axis=0)
             for x in range(4):
                 z = rot(tiles[0], -32 * x, 1)
                 z = jnp.where(group == 1, rot(tiles[1], 32 - 32 * x, 1), z)
@@ -294,31 +335,47 @@
 
 
 def kernel(
-    cls_ref, val_ref, cell_ref, rate_ref, guess_ref, p_ref, r_ref,
-    fr, vb, kf, g0, t0, c0, u0, sb2, rb2, sbv, rbv,
-    pair, w1, k1, b1, v1, q1, g1, t1, c1, sbk1, rbk1, sbb1, rbb1, sbv1, rbv1,
+    cls_hbm, val_hbm, cell_hbm, rate_hbm, guess_hbm, p_ref, r_ref,
+    cls_ref, val_ref, cell_ref, rate_ref, fr, vb, kf, g0, t0, c0, u0, sb2, rb2, sbv, rbv,
+    pair, w1, wk, k1, b1, v1, q1, g1, t1, c1, sbb1, rbb1, sbv1, rbv1,
     pair1, w2, k2, b2, v2, q2, g2, t2, c2, sbk2, rbk2, sbb2, rbb2,
-    pair2, k3, v3, q3, g3, t3, c3, exp3, exp2, exp1, send, recv,
+    pair2, k3, v3, q3, g3, t3, c3, exp3, exp2, exp1, send, recv, load,
 ):
     me = lax.axis_index("space")
+    loads = [
+        pltpu.make_async_copy(src, dst, load.at[i])
+        for i, (src, dst) in enumerate(
+            [
+                (cls_hbm.at[0], cls_ref),
+                (val_hbm, val_ref),
+                (guess_hbm.at[0], fr.at[pl.ds(4, 16), pl.ds(0, 16), pl.ds(0, 128)]),
+                (cell_hbm, cell_ref),
+                (rate_hbm, rate_ref),
+            ]
+        )
+    ]
+    for copy in loads:
+        copy.start()
     barrier = pltpu.get_barrier_semaphore()
-    for o in GATHER:
+    for o in NEAR:
         pl.semaphore_signal(
             barrier, inc=1, device_id={"space": lax.rem(me + o, N)}, device_id_type=pl.DeviceIdType.MESH
         )
 
+    for copy in loads:
+        copy.wait()
+    vals = [jnp.broadcast_to(val_ref[0:1, i : i + 1], (16, 128)) for i in range(8)]
+
     def lookup(x):
-        cls = cls_ref[0, x]
-        b0, b1_, b2_ = (cls & 1) == 0, (cls & 2) == 0, (cls & 4) == 0
-        pairs = [jnp.where(b0, val_ref[2 * i], val_ref[2 * i + 1]) for i in range(4)]
-        quads = [jnp.where(b1_, pairs[0], pairs[1]), jnp.where(b1_, pairs[2], pairs[3])]
-        kf[x + 4, 0:16, 0:128] = jnp.where(b2_, quads[0], quads[1])
-        fr[x + 4, 0:16, 0:128] = guess_ref[0, x]
+        cls = cls_ref[x]
+        bits = [(cls & 1) == 0, (cls & 2) == 0, (cls & 4) == 0]
+        pairs = [jnp.where(bits[0], vals[2 * i], vals[2 * i + 1]) for i in range(4)]
+        quads = [jnp.where(bits[1], pairs[0], pairs[1]), jnp.where(bits[1], pairs[2], pairs[3])]
+        kf[x + 4, 0:16, 0:128] = jnp.where(bits[2], quads[0], quads[1])
 
     layer_loop(0, 16, lookup)
     pack0(lambda a, x: (fr if a == 0 else kf)[x + 4, 0:16, 0:128], 2, sb2)
-
-    pl.semaphore_wait(barrier, len(GATHER))
+    pl.semaphore_wait(barrier, len(NEAR))
     send_plan(me, PLAN2, sb2, rb2, send.at[0], recv.at[0])
 
     def same(shape, f):
@@ -327,7 +384,7 @@
     pool0 = same((128, 128), lambda l, c: l // 2 == c % 64)
     pool1 = same((128, 128), lambda l, c: (l // 2 == c % 32) & (l < 64))
 
-    def coarsen0(layer):
+    def coarsen0(layer, w1):
         def body(x):
             pair[x] = layer(2 * x) + layer(2 * x + 1)
 
@@ -355,14 +412,9 @@
             s = 0.125 * pair_rows(pair2, x, 8)
             out[x] = s + jnp.where(even, pltpu.roll(s, 127, 1), pltpu.roll(s, 1, 1))
 
-    coarsen0(lambda x: kf[x + 4, 0:16, 0:128])
-    pack1(w1, sbk1)
-    send_plan(me, PLAN1, sbk1, rbk1, send.at[1], recv.at[1])
-    q1[0:8, 0:8] = w1[...]
-    coarsen1(w1, 0)
+    coarsen0(lambda x: kf[x + 4, 0:16, 0:128], wk)
+    coarsen1(wk, 0)
     pack2(w2, sbk2)
-    for o in GATHER:
-        start_to(me, sbk2, rbk2.at[SLOT[o]], send.at[2], recv.at[2], o)
 
     cell, rate = cell_ref[...], rate_ref[...]
     ix, iy, iz = cell // (64 * 512), cell // 512 % 64, cell % 512
@@ -395,14 +447,17 @@
     layer_loop(2, 22, coefs0)
     sweep0(fr, vb, g0, c0, 2, 22)
     sweep0(vb, u0, g0, c0, 3, 21)
-    coarsen0(lambda x: own_residual0(u0, g0, c0, t0, x + 4)[1])
-    pack1(w1, sbb1)
-    send_plan(me, PLAN1, sbb1, rbb1, send.at[3], recv.at[3])
+    coarsen0(lambda x: own_residual0(u0, g0, c0, t0, x + 4)[1], w1)
+    pack1([w1, wk], sbb1)
+    send_plan(me, PLANS1[2][0], sbb1, rbb1, send.at[1], recv.at[1])
+    for o in GATHER:
+        start_to(me, sbk2, rbk2.at[SLOT[o]], send.at[2], recv.at[2], o)
     pack0(lambda a, x: u0[x + 4, 0:16, 0:128], 1, sbv)
-    send_plan(me, PLANV, sbv, rbv, send.at[4], recv.at[4])
-
-    wait_got(rbk1, recv.at[1])
-    unpack1(q1, rbk1, k1)
+    wait_sent(rb2, send.at[0])
+
+    wait_got(rbb1, recv.at[1])
+    unpack1(1, 2, wk, rbb1, k1)
+    unpack1(0, 2, w1, rbb1, b1)
 
     def coefs1(x):
         k, near = shifts1(k1, x)
@@ -410,8 +465,37 @@
         for i in range(6):
             g1[i, x] = gs[i]
         t1[x] = 0.25 * total
+        c1[x] = OMEGA * b1[x] / t1[x]
 
     layer_loop(1, 15, coefs1)
+
+    def sweep1(cur, out, low, high):
+        def body(x):
+            v, near = shifts1(cur, x)
+            out[x] = v + change(v, near, [g1[i, x] for i in range(6)], c1[x])
+
+        layer_loop(low, high, body)
+
+    sweep1(c1, v1, 3, 13)
+
+    def down1(x):
+        v, near = shifts1(v1, x)
+        r = change(v, near, [g1[i, x] for i in range(6)], c1[x]) * t1[x]
+        q1[x] = (1.0 / OMEGA) * r[0:8]
+
+    layer_loop(4, 12, down1)
+    coarsen1(q1, 4)
+    pack2(w2, sbb2)
+    for o in GATHER:
+        start_to(me, sbb2, rbb2.at[SLOT[o]], send.at[3], recv.at[3], o)
+    half = lanes_of((8, 128)) < 64
+    for x in range(8):
+        v = v1[x + 4, 0:8]
+        w1[x] = jnp.where(half, v, pltpu.roll(v, 64, 1))
+    pack1([w1], sbv1)
+    send_plan(me, PLANS1[1][0], sbv1, rbv1, send.at[4], recv.at[4])
+    send_plan(me, PLANV, sbv, rbv, send.at[5], recv.at[5])
+
     rbk2[SLOT[0]] = sbk2[...]
     wait_got(rbk2.at[pl.ds(0, len(GATHER))], recv.at[2])
     unpack2(rbk2, k2)
@@ -441,53 +525,11 @@
 
     layer_loop(0, 8, coefs3)
 
-    wait_got(rbb1, recv.at[3])
-    unpack1(w1, rbb1, b1)
-
-    def first1(x):
-        c1[x] = OMEGA * b1[x] / t1[x]
-
-    layer_loop(1, 15, first1)
-
-    def sweep1(cur, out, low, high):
-        def body(x):
-            v, near = shifts1(cur, x)
-            out[x] = v + change(v, near, [g1[i, x] for i in range(6)], c1[x])
-
-        layer_loop(low, high, body)
-
-    sweep1(c1, v1, 3, 13)
-
-    def down1(x):
-        v, near = shifts1(v1, x)
-        r = change(v, near, [g1[i, x] for i in range(6)], c1[x]) * t1[x]
-        q1[x] = (1.0 / OMEGA) * r[0:8]
-
-    layer_loop(4, 12, down1)
-    coarsen1(q1, 4)
-    pack2(w2, sbb2)
-    for o in GATHER:
-        start_to(me, sbb2, rbb2.at[SLOT[o]], send.at[6], recv.at[6], o)
-    half = lanes_of((8, 128)) < 64
-    for x in range(8):
-        v = v1[x + 4, 0:8]
-        w1[x] = jnp.where(half, v, pltpu.roll(v, 64, 1))
-    pack1(w1, sbv1)
-    send_plan(me, PLAN1, sbv1, rbv1, send.at[5], recv.at[5])
-
-    wait_sent(rb2, send.at[0])
-    wait_sent(rbk1, send.at[1])
+    wait_sent(rbb1, send.at[1])
     wait_sent(rbk2.at[pl.ds(0, len(GATHER))], send.at[2])
-    wait_sent(rbb1, send.at[3])
-    wait_sent(rbv, send.at[4])
-    wait_got(rbv, recv.at[4])
-    unpack0(0, 1, PLANV, rbv, u0)
-    wait_got(rbv1, recv.at[5])
-    unpack1(w1, rbv1, v1)
-    wait_sent(rbv1, send.at[5])
 
     rbb2[SLOT[0]] = sbb2[...]
-    wait_got(rbb2.at[pl.ds(0, len(GATHER))], recv.at[6])
+    wait_got(rbb2.at[pl.ds(0, len(GATHER))], recv.at[3])
     unpack2(rbb2, b2)
 
     def first2(x):
@@ -541,6 +583,8 @@
     sweep2(q2, v2)
     sweep2(v2, q2)
 
+    wait_got(rbv1, recv.at[4])
+    unpack1(0, 1, w1, rbv1, v1)
     spread2 = same((128, 128), lambda c, f: c == jnp.where(f < 96, f // 2, 64 + f // 2))
     row = rows_of((8, 128))
     order = [14, 15, 0, 1, 2, 3, 4, 5]
@@ -555,6 +599,8 @@
     sweep1(b1, v1, 1, 15)
     sweep1(v1, b1, 2, 14)
 
+    wait_got(rbv, recv.at[5])
+    unpack0(0, 1, PLANV, rbv, u0)
     def spread(c, f):
         return c == jnp.where(f < 192, f // 2, f // 2)
 
@@ -586,7 +632,9 @@
         r_ref[0, x] = r
 
     layer_loop(0, 16, finish)
-    wait_sent(rbb2.at[pl.ds(0, len(GATHER))], send.at[6])
+    wait_sent(rbv1, send.at[4])
+    wait_sent(rbv, send.at[5])
+    wait_sent(rbb2.at[pl.ds(0, len(GATHER))], send.at[3])
 
 
 def shards(perm_class, class_values, well_cells, well_rates, guess):
@@ -602,23 +650,23 @@
     return pl.pallas_call(
         kernel,
         out_shape=(block, block),
-        in_specs=[vmem, pl.BlockSpec(memory_space=pltpu.SMEM), vmem, vmem, vmem],
+        in_specs=[pl.BlockSpec(memory_space=pltpu.HBM)] * 5,
         out_specs=(vmem, vmem),
         scratch_shapes=[
-            f(*l0), f(*l0), f(*l0), f(6, *l0), f(*l0), f(*l0), f(*l0),
+            pltpu.VMEM(guess.shape[1:], jnp.int32), f(1, 8), pltpu.VMEM((1, wells), jnp.int32), f(1, wells), f(*l0), f(*l0), f(*l0), f(6, *l0), f(*l0), f(*l0), f(*l0),
             f(SEND2, *t), f(GOT2, *t), f(SENDV, *t), f(GOTV, *t),
-            f(8, 16, 128), f(8, *t), f(*l1), f(*l1), f(*l1), f(16, *t), f(6, *l1), f(*l1), f(*l1),
-            f(SEND1, *t), f(GOT1, *t), f(SEND1, *t), f(GOT1, *t), f(SEND1, *t), f(GOT1, *t),
+            f(8, 16, 128), f(8, *t), f(8, *t), f(*l1), f(*l1), f(*l1), f(16, *t), f(6, *l1), f(*l1), f(*l1),
+            *[f(n, *t) for narr in (2, 1) for n in PLANS1[narr][1:]],
             f(4, *t), f(4, *t), f(*l2), f(*l2), f(*l2), f(*l2), f(6, *l2), f(*l2), f(*l2),
-            f(*t), f(len(GATHER) + 1, *t), f(*t), f(len(GATHER) + 1, *t),
+            f(4, 128), f(len(GATHER) + 1, 4, 128), f(4, 128), f(len(GATHER) + 1, 4, 128),
             f(8, 16, 128), f(*l3), f(*l3), f(*l3), f(6, *l3), f(*l3), f(*l3),
             f(8, 16, 128), f(8, 16, 128), f(12, 2, 32, 128),
-            pltpu.SemaphoreType.DMA((7,)), pltpu.SemaphoreType.DMA((7,)),
+            pltpu.SemaphoreType.DMA((6,)), pltpu.SemaphoreType.DMA((6,)), pltpu.SemaphoreType.DMA((5,)),
         ],
         compiler_params=pltpu.CompilerParams(
             collective_id=0, has_side_effects=True, vmem_limit_bytes=40 * 1024 * 1024
         ),
-    )(perm_class, class_values, well_cells.reshape(1, wells), well_rates.reshape(1, wells), guess)
+    )(*[pltpu.with_memory_space_constraint(q, pltpu.HBM) for q in (perm_class, class_values.reshape(1, 8), well_cells.reshape(1, wells), well_rates.reshape(1, wells), guess)])
 
 
 def solution(mesh):

time: 50.3 us -> 41.4 us (0.82)
  Pallas kernels: 45.7 us -> 39.4 us
  local copies, waits for them, and re-layouts: 3.78 us -> 1.31 us
    pallas_call x1, Pallas kernels: 45.7 us -> 39.4 us  [shards(): pl.pallas_call(kernel, out_shape=(block, block), in_specs=[pl.BlockSpec(m...]
    unnamed x12 -> x2, local copies, waits for them, and re-layouts: 3.78 us -> 1.31 us
where the time goes in v3:
time: 41.4 us; the launch traced here: 41.3 us
  Pallas kernels  39.4 us (95%)
  local copies, waits for them, and re-layouts  1.31 us (3%)
  between operations  0.64 us (2%)
    pallas_call x1, Pallas kernels, shards(): pl.pallas_call(kernel, out_shape=(block, block), in_specs=[pl.BlockSpec(m...  39.4 us
    unnamed x2, local copies, waits for them, and re-layouts  1.31 us

profile of v3, /device:TPU:2, one launch (start us, length us, event | category | flops | bytes accessed | tf_op | source)
XLA Modules:
  0.0 41.3 jit_solution(12954290787284763583)
XLA Ops:
  0.6 39.4 %shard_map.68 = (f32[1,16,16,128]{3,2,1,0:T(8,128)S(1)}, f32[1,16,16,128]{3,2,1,0:T(8,128)S(1)}) custom-call(s32[1,16,16,128]{3,2,1,0:T(8,128)} %cls_hbm.1, f32[1,8]{1,0:T(1,128)} %bitcast.3, s32[1,16]{1,0:T(1,128)} %bitcast.4, f32[1,16]{1,0:T(1,128)} %bitcast.5, f32[1,16,16,128]{3,2,1,0:T(8,128)} %guess_hbm.1), custom_call_target="tpu_custom_call" | custom-call | tf_op jit(solution)/shard_map/pallas_call | solution.py:650
  40.0 0.7 %copy.9 = f32[1,16,16,128]{3,2,1,0:T(8,128)} copy(f32[1,16,16,128]{3,2,1,0:T(8,128)S(1)} %get-tuple-element.4) | data formatting | bytes 262144
  40.7 0.7 %copy.10 = f32[1,16,16,128]{3,2,1,0:T(8,128)} copy(f32[1,16,16,128]{3,2,1,0:T(8,128)S(1)} %get-tuple-element.5) | data formatting | bytes 262144

commit v4 on v3

--- a/solution.py
+++ b/solution.py
@@ -32,8 +32,8 @@
     x_at = {1: 0, -1: 6 * narr}
     y_at = {1: 12 * narr, -1: 20 * narr}
     e_at = {d: 28 * narr + i for i, d in enumerate([(1, 1), (1, -1), (-1, 1), (-1, -1)])}
-    z_at = {1: 28 * narr + 4, -1: 28 * narr + 6}
-    return x_at, y_at, e_at, z_at, 28 * narr + 8
+    z_at = {1: 28 * narr + 4, -1: 29 * narr + 4}
+    return x_at, y_at, e_at, z_at, 30 * narr + 4
 
 
 def plan0(narr):
@@ -41,8 +41,10 @@
     plan, got = {}, 0
     for d in DIRS:
         dx, dy, dz = d
+        if dy and dz:
+            continue
         if dz:
-            src, count = z_at[dz] + (1 if dy < 0 else 0), 2 if dy == 0 else 1
+            src, count = z_at[dz], narr
         elif dx and dy:
             src, count = e_at[(dx, dy)], 1
         elif dy:
@@ -54,29 +56,40 @@
     return plan, length, got
 
 
-def plan1(narr):
+def plan1():
     plan, got = {}, 0
     for d in DIRS:
         dx, dy, dz = d
         if dz:
-            src, count = 8 * narr, 1
-        elif dy:
-            src = (4 if dy > 0 else 6) * narr + (narr if dx < 0 else 0)
-            count = narr if dx else 2 * narr
-        else:
-            src, count = (0 if dx > 0 else 2 * narr), 2 * narr
+            continue
+        src, count = (1 if dx < 0 else 0, 3) if dx else (0, 4)
         plan[d] = (src, got, count)
         got += count
-    return plan, 8 * narr + 1, got
+    return plan, 4, got
 
 
 PLAN2, SEND2, GOT2 = plan0(2)
 PLANV, SENDV, GOTV = plan0(1)
-PLANS1 = {n: plan1(n) for n in (1, 2)}
+PLAN1, SEND1, GOT1 = plan1()
+SIDE2 = {(dz, dy): i for i, (dz, dy) in enumerate([(1, 1), (1, -1), (-1, 1), (-1, -1)])}
+EDGE0 = {d: (SIDE2[(d[2], d[1])], i, 1) for i, d in enumerate(d for d in DIRS if d[1] and d[2])}
+ENDS1 = {d: ((1 - d[2]) // 2, i, 1) for i, d in enumerate(d for d in DIRS if d[2])}
 NEAR = sorted((offset(d) for d in DIRS), key=lambda o: (-hops(o), o))
 GATHER = sorted((o for o in range(1, N) if o % 4 != 2), key=lambda o: (-hops(o), o))
 SLOT = {o: i for i, o in enumerate(GATHER)}
 SLOT[0] = len(GATHER)
+
+
+def plan2():
+    places, got = {}, 0
+    for o in GATHER + [0]:
+        side = {0: 0, 1: 1, 3: -1}[o % 4]
+        places[o] = (0, got, 2) if side == 0 else (2 if side > 0 else 3, got, 1)
+        got += places[o][2]
+    return places, got
+
+
+PART2, PARTS = plan2()
 
 
 def rows_of(shape):
@@ -111,10 +124,14 @@
     ).start()
 
 
-def send_plan(me, plan, sb, rb, send, recv):
-    for d in sorted(plan, key=lambda d: -hops(offset(d))):
-        src, got, count = plan[d]
-        start_to(me, sb.at[pl.ds(src, count)], rb.at[pl.ds(got, count)], send, recv, offset(d))
+def send_plan(me, plan, small, sb, rb, se, re, send, recv, i):
+    for d in sorted(DIRS, key=lambda d: -hops(offset(d))):
+        for messages, src, dst, sem in ((plan, sb, rb, i), (small, se, re, i + 1)):
+            if d in messages:
+                first, got, count = messages[d]
+                start_to(
+                    me, src.at[pl.ds(first, count)], dst.at[pl.ds(got, count)], send.at[sem], recv.at[sem], offset(d)
+                )
 
 
 def wait_got(rb, recv):
@@ -125,7 +142,7 @@
     pltpu.make_async_copy(rb, rb, send).wait()
 
 
-def pack0(own, narr, sb):
+def pack0(own, narr, sb, se):
     x_at, y_at, e_at, z_at, _ = sent0(narr)
     low4 = rows_of((8, 128)) < 4
     two = rows_of((8, 128)) // 2
@@ -155,11 +172,16 @@
             zlo = jnp.where(group == g, rot(v, 4 * g, 1), zlo)
             zhi = jnp.where(group == g, rot(v, 4 * g + 4, 1), zhi)
     for side, z in ((1, zlo), (-1, zhi)):
-        sb[z_at[side]] = z[0:8]
-        sb[z_at[side] + 1] = z[8:16]
-
-
-def unpack0(a, narr, plan, rb, out):
+        if narr == 2:
+            sb[z_at[side]] = z[0:8]
+            sb[z_at[side] + 1] = z[8:16]
+        else:
+            sb[z_at[side]] = jnp.where(lanes_of((8, 128)) < 64, z[0:8], rot(z[8:16], 64, 1))
+        se[SIDE2[(side, 1)]] = z[0:2]
+        se[SIDE2[(side, -1)]] = z[14:16]
+
+
+def unpack0(a, narr, plan, rb, re, out):
     low4 = rows_of((8, 128)) < 4
 
     def at(d):
@@ -184,8 +206,9 @@
         parts = {}
         for dz in (1, -1):
             mid = at((dx, 0, dz))
-            tail = jnp.where(low4, rb[at((dx, 1, dz))], rb[at((dx, -1, dz))])
-            parts[dz] = jnp.concatenate([rb[mid], rb[mid + 1], tail], axis=0)
+            up, lo = re[EDGE0[(dx, 1, dz)][1]], re[EDGE0[(dx, -1, dz)][1]]
+            last = rb[mid + 1] if narr == 2 else rot(rb[mid], 64, 1)
+            parts[dz] = jnp.concatenate([rb[mid], last, up, up, lo, lo], axis=0)
         for x in layers:
             g = 16 * a + (x - 4) % 16
             out[x, :, 128:256] = jnp.where(half, rot(parts[1], -4 * g, 1), rot(parts[-1], 124 - 4 * g, 1))
@@ -229,54 +252,33 @@
     return v, r[0:16, 0:128]
 
 
-def pack1(ws, sb):
-    narr = len(ws)
-    half, low4 = lanes_of((8, 128)) < 64, rows_of((8, 128)) < 4
-    group = lanes_of((8, 128)) // 4
-    z = jnp.zeros((8, 128), F32)
-    for a, w in enumerate(ws):
-        for j in range(4):
-            sb[j * narr + a] = jnp.where(half, w[2 * j], w[2 * j + 1])
-        for j in range(2):
-            p, q, r, t = (w[4 * j + i] for i in range(4))
-            here, there = jnp.where(half, p, r), rot(jnp.where(half, q, t), 4, 0)
-            sb[(4 + j) * narr + a] = jnp.where(low4, here, there)
-            sb[(6 + j) * narr + a] = jnp.where(low4, there, here)
+def pack1(w, sb, se):
+    half, group = lanes_of((8, 128)) < 64, lanes_of((8, 128)) // 8
+    for j in range(4):
+        sb[j] = jnp.where(half, w[2 * j], w[2 * j + 1])
+    for i in range(2):
+        z = jnp.zeros((8, 128), F32)
         for x in range(8):
-            g = 16 * a + x
-            z = jnp.where(group == g, rot(w[x], 4 * g, 1), z)
-            z = jnp.where(group == g + 8, rot(w[x], 4 * (g + 8) - 60, 1), z)
-    sb[8 * narr] = z
-
-
-def unpack1(a, narr, w, rb, out):
+            z = jnp.where(group == x, rot(w[x], 8 * x - 56 * i, 1), z)
+        se[i] = jnp.where(half, z, rot(rot(z, 4, 0), 64, 1))[0:4]
+
+
+def unpack1(w, rb, re, out):
     half, quarter = lanes_of((8, 128)) < 64, lanes_of((8, 128)) < 96
-    low4 = rows_of((8, 128)) < 4
-    plan = PLANS1[narr][0]
-
-    def at(d, j=0):
-        return rb[plan[d][1] + j * narr + a]
-
-    def layer(dx, x):
-        if dx == 0:
+
+    def block(dx, dy, x):
+        if (dx, dy) == (0, 0):
             return w[x]
-        tile = at((dx, 0, 0), x // 2 - (2 if dx < 0 else 0))
+        tile = rb[PLAN1[(dx, dy, 0)][1] + x // 2 - (1 if dx < 0 else 0)]
         return rot(tile, 64, 1) if x % 2 else tile
 
-    def rows(dx, x):
-        j = x // 4 if dx == 0 else 0
-        up, lo = at((dx, 1, 0), j), at((dx, -1, 0), j)
-        tile = rot(jnp.where(low4, lo, up), 4, 0) if x % 2 else jnp.where(low4, up, lo)
-        return rot(tile, 64, 1) if x % 4 > 1 else tile
-
-    for dx, layers in ((0, range(8)), (1, range(4)), (-1, range(4, 8))):
-        tail = {dz: rb[plan[(dx, 0, dz)][1]] for dz in (1, -1)}
-        tail1 = {dz: jnp.where(low4, rb[plan[(dx, 1, dz)][1]], rb[plan[(dx, -1, dz)][1]]) for dz in (1, -1)}
-        for x in layers:
-            g = 16 * a + x
-            ends = [jnp.where(quarter, rot(q[1], 64 - 4 * g, 1), rot(q[-1], 124 - 4 * (g + 8), 1)) for q in (tail, tail1)]
-            out[4 + x + 8 * dx, 0:8] = jnp.where(half, layer(dx, x), ends[0])
-            out[4 + x + 8 * dx, 8:16] = jnp.where(half, rows(dx, x), ends[1])
+    for dx, layers in ((0, range(8)), (1, range(6)), (-1, range(2, 8))):
+        for t, dy in enumerate((0, 1, -1)):
+            up, lo = re[ENDS1[(dx, dy, 1)][1]], re[ENDS1[(dx, dy, -1)][1]]
+            up, lo = (jnp.concatenate([q, rot(q, 64, 1)], axis=0) for q in (up, lo))
+            for x in layers:
+                ends = jnp.where(quarter, rot(up, 64 - 8 * x, 1), rot(lo, 120 - 8 * x, 1))
+                out[6 + x + 8 * dx, 8 * t : 8 * t + 8] = jnp.where(half, block(dx, dy, x), ends)
 
 
 def shifts1(ref, x):
@@ -285,7 +287,7 @@
         ref[x - 1],
         ref[x + 1],
         pltpu.roll(v, 1, 0),
-        pltpu.roll(v, 15, 0),
+        pltpu.roll(v, 23, 0),
         pltpu.roll(v, 1, 1),
         pltpu.roll(v, 127, 1),
     )
@@ -330,15 +332,78 @@
                 out[4 * cx + x, 8 * t : 8 * t + 8] = z
 
 
+def pack_parts(main, ends, low, high, sb):
+    lane = lanes_of((8, 128))
+    inner = main[1]
+    outer = jnp.where(lane < 32, main[0], main[5])
+    up, lo = low[0], high[0]
+    for x in range(1, 4):
+        inner = jnp.where(lane // 32 == x, main[x + 1], inner)
+    for x in range(1, 6):
+        up = jnp.where(lane // 16 == x, low[x], up)
+        lo = jnp.where(lane // 16 == x, high[x], lo)
+    for x in range(6):
+        outer = jnp.where((lane == 97 + 2 * x) | (lane == 112 + 2 * x), ends[x], outer)
+        up = jnp.where(lane == 96 + 2 * x, ends[x], up)
+        lo = jnp.where(lane == 113 + 2 * x, ends[x], lo)
+    for i, tile in enumerate((inner, outer, up, lo)):
+        sb[i] = tile
+
+
+def sum_parts(rb, out):
+    lane, row = lanes_of((8, 128)), rows_of((8, 128))
+    odd = lane % 2 == 1
+
+    def column(cx, cy):
+        first = PART2[(16 * cx + 4 * cy) % N][1]
+        inner, outer = rb[first], rb[first + 1]
+        up = rb[PART2[(16 * cx + 4 * cy + 1) % N][1]]
+        lo = rb[PART2[(16 * cx + 4 * cy - 1) % N][1]]
+        above, below = jnp.where(odd, outer, up), jnp.where(odd, lo, outer)
+        layers = []
+        for x in range(6):
+            own = rot(inner, -32 * (x - 1), 1) if 0 < x < 5 else rot(outer, -32 * (x // 5), 1)
+            z = jnp.where(lane < 48, rot(up, 32 - 16 * x, 1), rot(lo, 112 - 16 * x, 1))
+            z = jnp.where((lane >= 48) & (lane < 112), 0.0, z)
+            z = jnp.where(lane < 32, own, z)
+            e = jnp.where((lane == 31) | (lane == 32), rot(above, 31 - 96 - 2 * x, 1), 0.0)
+            e = jnp.where((lane == 127) | (lane == 0), rot(below, 15 - 2 * x, 1), e)
+            layers.append(z + e)
+        return layers
+
+    even = {(cx, t): column(cx, 2 * t) for cx in range(4) for t in range(2)}
+    turned = {
+        (cx, t): [pltpu.roll(q, 4, 0) for q in column(cx, 2 * t + 1)] for cx in range(4) for t in range(2)
+    }
+    rows = {}
+    for cx in range(4):
+        for t in range(2):
+            after = even[(cx, 1) if t == 0 else ((cx + 1) % 4, 0)]
+            before = turned[(cx, 0) if t == 1 else ((cx - 1) % 4, 1)]
+            rows[(cx, t)] = [
+                jnp.where(row < 5, even[(cx, t)][x], after[x]) + jnp.where(row >= 3, turned[(cx, t)][x], before[x])
+                for x in range(6)
+            ]
+    for cx in range(4):
+        for t in range(2):
+            for x in range(4):
+                z = rows[(cx, t)][x + 1]
+                if x == 0:
+                    z = z + rows[((cx - 1) % 4, t)][5]
+                if x == 3:
+                    z = z + rows[((cx + 1) % 4, t)][0]
+                out[4 * cx + x, 8 * t : 8 * t + 8] = z
+
+
 def pair_rows(ref, index, count):
     return ref[index, pl.ds(0, count, stride=2), :] + ref[index, pl.ds(1, count, stride=2), :]
 
 
 def kernel(
     cls_hbm, val_hbm, cell_hbm, rate_hbm, guess_hbm, p_ref, r_ref,
-    cls_ref, val_ref, cell_ref, rate_ref, fr, vb, kf, g0, t0, c0, u0, sb2, rb2, sbv, rbv,
-    pair, w1, wk, k1, b1, v1, q1, g1, t1, c1, sbb1, rbb1, sbv1, rbv1,
-    pair1, w2, k2, b2, v2, q2, g2, t2, c2, sbk2, rbk2, sbb2, rbb2,
+    cls_ref, val_ref, cell_ref, rate_ref, fr, vb, kf, g0, t0, c0, u0, sb2, rb2, sbv, rbv, se2, re2, sev, rev,
+    pair, w1, wk, k1, b1, v1, g1, t1, c1, sbk1, rbk1, sbb1, rbb1, sek1, rek1, seb1, reb1,
+    pair1, part, w2, k2, b2, v2, q2, g2, t2, c2, sbk2, rbk2, sbb2, rbb2,
     pair2, k3, v3, q3, g3, t3, c3, exp3, exp2, exp1, send, recv, load,
 ):
     me = lax.axis_index("space")
@@ -357,7 +422,7 @@
     for copy in loads:
         copy.start()
     barrier = pltpu.get_barrier_semaphore()
-    for o in NEAR:
+    for o in GATHER:
         pl.semaphore_signal(
             barrier, inc=1, device_id={"space": lax.rem(me + o, N)}, device_id_type=pl.DeviceIdType.MESH
         )
@@ -374,9 +439,9 @@
         kf[x + 4, 0:16, 0:128] = jnp.where(bits[2], quads[0], quads[1])
 
     layer_loop(0, 16, lookup)
-    pack0(lambda a, x: (fr if a == 0 else kf)[x + 4, 0:16, 0:128], 2, sb2)
-    pl.semaphore_wait(barrier, len(NEAR))
-    send_plan(me, PLAN2, sb2, rb2, send.at[0], recv.at[0])
+    pack0(lambda a, x: (fr if a == 0 else kf)[x + 4, 0:16, 0:128], 2, sb2, se2)
+    pl.semaphore_wait(barrier, len(GATHER))
+    send_plan(me, PLAN2, EDGE0, sb2, rb2, se2, re2, send, recv, 0)
 
     def same(shape, f):
         return f(rows_of(shape), lanes_of(shape)).astype(F32)
@@ -405,6 +470,12 @@
 
     even = lanes_of((8, 128)) % 2 == 0
 
+    def pool_parts(l, c):
+        z = jnp.where(l < 64, l // 2, jnp.where(l < 66, 32, jnp.where(l >= 126, -1, -2)))
+        main, ends = z == c % 32, z == jnp.where(c % 2 == 0, -1, 32)
+        low, high = z == c % 16, z == 16 + c % 16
+        return ((c < 128) & main) | ((c // 128 == 1) & ends) | ((c // 128 == 2) & low) | ((c // 128 == 3) & high)
+
     def coarsen2(ref, out):
         for x in range(8):
             pair2[x] = ref[2 * x] + ref[2 * x + 1]
@@ -413,8 +484,12 @@
             out[x] = s + jnp.where(even, pltpu.roll(s, 127, 1), pltpu.roll(s, 1, 1))
 
     coarsen0(lambda x: kf[x + 4, 0:16, 0:128], wk)
+    pack1(wk, sbk1, sek1)
+    send_plan(me, PLAN1, ENDS1, sbk1, rbk1, sek1, rek1, send, recv, 2)
     coarsen1(wk, 0)
     pack2(w2, sbk2)
+    for o in GATHER:
+        start_to(me, sbk2, rbk2.at[SLOT[o]], send.at[8], recv.at[8], o)
 
     cell, rate = cell_ref[...], rate_ref[...]
     ix, iy, iz = cell // (64 * 512), cell // 512 % 64, cell % 512
@@ -433,8 +508,9 @@
     ).reshape(24, 24, 256)
 
     wait_got(rb2, recv.at[0])
-    unpack0(0, 2, PLAN2, rb2, fr)
-    unpack0(1, 2, PLAN2, rb2, kf)
+    wait_got(re2, recv.at[1])
+    unpack0(0, 2, PLAN2, rb2, re2, fr)
+    unpack0(1, 2, PLAN2, rb2, re2, kf)
 
     def coefs0(x):
         k, near = shifts0(kf, x)
@@ -448,16 +524,17 @@
     sweep0(fr, vb, g0, c0, 2, 22)
     sweep0(vb, u0, g0, c0, 3, 21)
     coarsen0(lambda x: own_residual0(u0, g0, c0, t0, x + 4)[1], w1)
-    pack1([w1, wk], sbb1)
-    send_plan(me, PLANS1[2][0], sbb1, rbb1, send.at[1], recv.at[1])
-    for o in GATHER:
-        start_to(me, sbk2, rbk2.at[SLOT[o]], send.at[2], recv.at[2], o)
-    pack0(lambda a, x: u0[x + 4, 0:16, 0:128], 1, sbv)
-    wait_sent(rb2, send.at[0])
-
-    wait_got(rbb1, recv.at[1])
-    unpack1(1, 2, wk, rbb1, k1)
-    unpack1(0, 2, w1, rbb1, b1)
+
+    own1 = lanes_of((8, 128)) < 64
+
+    def part1(x):
+        b1[x] = jnp.zeros((24, 128), F32)
+        v1[x] = jnp.zeros((24, 128), F32)
+
+    layer_loop(3, 17, part1)
+    wait_got(rbk1, recv.at[2])
+    wait_got(rek1, recv.at[3])
+    unpack1(wk, rbk1, rek1, k1)
 
     def coefs1(x):
         k, near = shifts1(k1, x)
@@ -465,39 +542,51 @@
         for i in range(6):
             g1[i, x] = gs[i]
         t1[x] = 0.25 * total
-        c1[x] = OMEGA * b1[x] / t1[x]
-
-    layer_loop(1, 15, coefs1)
-
-    def sweep1(cur, out, low, high):
+
+    layer_loop(1, 19, coefs1)
+    for x in range(8):
+        b1[6 + x, 0:8] = jnp.where(own1, OMEGA * w1[x] / t1[6 + x, 0:8], 0.0)
+
+    def sweep1(cur, out, c, low, high):
         def body(x):
             v, near = shifts1(cur, x)
-            out[x] = v + change(v, near, [g1[i, x] for i in range(6)], c1[x])
+            out[x] = v + change(v, near, [g1[i, x] for i in range(6)], c[x])
 
         layer_loop(low, high, body)
 
-    sweep1(c1, v1, 3, 13)
+    sweep1(b1, v1, b1, 5, 15)
+    low4 = rows_of((8, 128)) < 4
 
     def down1(x):
         v, near = shifts1(v1, x)
-        r = change(v, near, [g1[i, x] for i in range(6)], c1[x]) * t1[x]
-        q1[x] = (1.0 / OMEGA) * r[0:8]
-
-    layer_loop(4, 12, down1)
-    coarsen1(q1, 4)
-    pack2(w2, sbb2)
-    for o in GATHER:
-        start_to(me, sbb2, rbb2.at[SLOT[o]], send.at[3], recv.at[3], o)
-    half = lanes_of((8, 128)) < 64
-    for x in range(8):
-        v = v1[x + 4, 0:8]
-        w1[x] = jnp.where(half, v, pltpu.roll(v, 64, 1))
-    pack1([w1], sbv1)
-    send_plan(me, PLANS1[1][0], sbv1, rbv1, send.at[4], recv.at[4])
-    send_plan(me, PLANV, sbv, rbv, send.at[5], recv.at[5])
+        return change(v, near, [g1[i, x] for i in range(6)], b1[x]) * t1[x]
+
+    for i in range(6):
+        q = down1(4 + 2 * i) + down1(5 + 2 * i)
+        part[i, 0:8] = q[0:8]
+        part[i, 8:16] = jnp.where(low4, q[8:16], q[16:24])
+    sums = jnp.concatenate([pair_rows(part, x, 8) for x in range(6)], axis=0)
+    wide = same((128, 512), pool_parts)
+    out = jnp.dot((0.125 / OMEGA) * sums, wide, precision=HI, preferred_element_type=F32)
+    pieces = [[out[8 * x : 8 * x + 8, 128 * i : 128 * i + 128] for x in range(6)] for i in range(4)]
+    pack_parts(*pieces, sbb2)
+
+    def gather(offsets):
+        for o in offsets:
+            src, got, count = PART2[o]
+            start_to(me, sbb2.at[pl.ds(src, count)], rbb2.at[pl.ds(got, count)], send.at[9], recv.at[9], o)
+
+    gather(GATHER[:24])
+    pack1(w1, sbb1, seb1)
+    send_plan(me, PLAN1, ENDS1, sbb1, rbb1, seb1, reb1, send, recv, 4)
+    gather(GATHER[24:])
+    pack0(lambda a, x: u0[x + 4, 0:16, 0:128], 1, sbv, sev)
+    send_plan(me, PLANV, EDGE0, sbv, rbv, sev, rev, send, recv, 6)
+    for i, buffer in enumerate((rb2, re2, rbk1, rek1)):
+        wait_sent(buffer, send.at[i])
 
     rbk2[SLOT[0]] = sbk2[...]
-    wait_got(rbk2.at[pl.ds(0, len(GATHER))], recv.at[2])
+    wait_got(rbk2.at[pl.ds(0, len(GATHER))], recv.at[8])
     unpack2(rbk2, k2)
     outside = lanes_of((16, 128)) // 32 == 2
 
@@ -525,12 +614,24 @@
 
     layer_loop(0, 8, coefs3)
 
-    wait_sent(rbb1, send.at[1])
-    wait_sent(rbk2.at[pl.ds(0, len(GATHER))], send.at[2])
-
-    rbb2[SLOT[0]] = sbb2[...]
-    wait_got(rbb2.at[pl.ds(0, len(GATHER))], recv.at[3])
-    unpack2(rbb2, b2)
+    wait_sent(rbk2.at[pl.ds(0, len(GATHER))], send.at[8])
+
+    wait_got(rbb1, recv.at[4])
+    wait_got(reb1, recv.at[5])
+    unpack1(w1, rbb1, reb1, b1)
+
+    def first1(x):
+        c1[x] = OMEGA * b1[x] / t1[x]
+
+    layer_loop(1, 19, first1)
+    sweep1(c1, v1, c1, 2, 18)
+    wait_sent(rbb1, send.at[4])
+    wait_sent(reb1, send.at[5])
+
+    for i in range(2):
+        rbb2[PARTS - 2 + i] = sbb2[i]
+    wait_got(rbb2.at[pl.ds(0, PARTS - 2)], recv.at[9])
+    sum_parts(rbb2, b2)
 
     def first2(x):
         c2[x] = OMEGA * jnp.where(outside, 0.0, b2[x]) / t2[x]
@@ -583,8 +684,6 @@
     sweep2(q2, v2)
     sweep2(v2, q2)
 
-    wait_got(rbv1, recv.at[4])
-    unpack1(0, 1, w1, rbv1, v1)
     spread2 = same((128, 128), lambda c, f: c == jnp.where(f < 96, f // 2, 64 + f // 2))
     row = rows_of((8, 128))
     order = [14, 15, 0, 1, 2, 3, 4, 5]
@@ -594,27 +693,23 @@
         e = out[8 * i : 8 * i + 8]
         exp2[i, pl.ds(0, 8, stride=2), :] = e
         exp2[i, pl.ds(1, 8, stride=2), :] = e
-    for x in range(16):
-        b1[x] = v1[x] + exp2[x // 2]
-    sweep1(b1, v1, 1, 15)
-    sweep1(v1, b1, 2, 14)
-
-    wait_got(rbv, recv.at[5])
-    unpack0(0, 1, PLANV, rbv, u0)
-    def spread(c, f):
-        return c == jnp.where(f < 192, f // 2, f // 2)
-
-    spread1 = same((128, 256), spread)
-    inside = (lanes_of((16, 128)) < 66) | (lanes_of((16, 128)) >= 126)
-    rows = [jnp.where(inside, b1[x], 0.0) for x in range(2, 14)]
+    for x in range(2, 18):
+        b1[x, 0:16] = v1[x, 0:16] + exp2[(x - 2) // 2]
+        b1[x, 16:24] = v1[x, 16:24] + exp2[(x - 2) // 2, 8:16]
+    sweep1(b1, v1, c1, 3, 17)
+    sweep1(v1, b1, c1, 4, 16)
+
+    wait_got(rbv, recv.at[6])
+    wait_got(rev, recv.at[7])
+    unpack0(0, 1, PLANV, rbv, rev, u0)
+    spread1 = same((128, 256), lambda c, f: c == f // 2)
+    rows = [q for x in range(4, 16) for q in (b1[x, 0:8], jnp.where(low4, b1[x, 8:16], b1[x, 16:24]))]
     out = jnp.dot(jnp.concatenate(rows, axis=0), spread1, precision=HI, preferred_element_type=F32)
-    low4 = rows_of((8, 256)) < 4
     for i in range(12):
         for h in range(2):
             e = out[16 * i : 16 * i + 16, 128 * h : 128 * h + 128]
             exp1[i, h, pl.ds(0, 16, stride=2), :] = e
             exp1[i, h, pl.ds(1, 16, stride=2), :] = e
-    low4 = rows_of((8, 128)) < 4
     for i in range(12):
         for h in range(2):
             tail = jnp.where(low4, exp1[i, h, 16:24], exp1[i, h, 24:32])
@@ -632,9 +727,9 @@
         r_ref[0, x] = r
 
     layer_loop(0, 16, finish)
-    wait_sent(rbv1, send.at[4])
-    wait_sent(rbv, send.at[5])
-    wait_sent(rbb2.at[pl.ds(0, len(GATHER))], send.at[3])
+    wait_sent(rbv, send.at[6])
+    wait_sent(rev, send.at[7])
+    wait_sent(rbb2.at[pl.ds(0, PARTS - 2)], send.at[9])
 
 
 def shards(perm_class, class_values, well_cells, well_rates, guess):
@@ -644,7 +739,7 @@
         return pltpu.VMEM(shape, F32)
 
     t = (8, 128)
-    l0, l1, l2, l3 = (24, 24, 256), (16, 16, 128), (16, 16, 128), (8, 8, 128)
+    l0, l1, l2, l3 = (24, 24, 256), (20, 24, 128), (16, 16, 128), (8, 8, 128)
     vmem = pl.BlockSpec(memory_space=pltpu.VMEM)
     block = jax.ShapeDtypeStruct(guess.shape, F32)
     return pl.pallas_call(
@@ -654,14 +749,14 @@
         out_specs=(vmem, vmem),
         scratch_shapes=[
             pltpu.VMEM(guess.shape[1:], jnp.int32), f(1, 8), pltpu.VMEM((1, wells), jnp.int32), f(1, wells), f(*l0), f(*l0), f(*l0), f(6, *l0), f(*l0), f(*l0), f(*l0),
-            f(SEND2, *t), f(GOT2, *t), f(SENDV, *t), f(GOTV, *t),
-            f(8, 16, 128), f(8, *t), f(8, *t), f(*l1), f(*l1), f(*l1), f(16, *t), f(6, *l1), f(*l1), f(*l1),
-            *[f(n, *t) for narr in (2, 1) for n in PLANS1[narr][1:]],
-            f(4, *t), f(4, *t), f(*l2), f(*l2), f(*l2), f(*l2), f(6, *l2), f(*l2), f(*l2),
-            f(4, 128), f(len(GATHER) + 1, 4, 128), f(4, 128), f(len(GATHER) + 1, 4, 128),
+            f(SEND2, *t), f(GOT2, *t), f(SENDV, *t), f(GOTV, *t), *([f(4, 2, 128), f(len(EDGE0), 2, 128)] * 2),
+            f(8, 16, 128), f(8, *t), f(8, *t), f(*l1), f(*l1), f(*l1), f(6, *l1), f(*l1), f(*l1),
+            *([f(SEND1, *t), f(GOT1, *t)] * 2), *([f(2, 4, 128), f(len(ENDS1), 4, 128)] * 2),
+            f(4, *t), f(6, 16, 128), f(4, *t), f(*l2), f(*l2), f(*l2), f(*l2), f(6, *l2), f(*l2), f(*l2),
+            f(4, 128), f(len(GATHER) + 1, 4, 128), f(4, *t), f(PARTS, *t),
             f(8, 16, 128), f(*l3), f(*l3), f(*l3), f(6, *l3), f(*l3), f(*l3),
             f(8, 16, 128), f(8, 16, 128), f(12, 2, 32, 128),
-            pltpu.SemaphoreType.DMA((6,)), pltpu.SemaphoreType.DMA((6,)), pltpu.SemaphoreType.DMA((5,)),
+            pltpu.SemaphoreType.DMA((10,)), pltpu.SemaphoreType.DMA((10,)), pltpu.SemaphoreType.DMA((5,)),
         ],
         compiler_params=pltpu.CompilerParams(
             collective_id=0, has_side_effects=True, vmem_limit_bytes=40 * 1024 * 1024

time: 41.4 us -> 40.2 us (0.971)
  Pallas kernels: 39.4 us -> 38.2 us
    pallas_call x1, Pallas kernels: 39.4 us -> 38.2 us  [shards(): pl.pallas_call(kernel, out_shape=(block, block), in_specs=[pl.BlockSpec(m...]
where the time goes in v4:
time: 40.2 us; the launch traced here: 40.1 us
  Pallas kernels  38.2 us (95%)
  local copies, waits for them, and re-layouts  1.31 us (3%)
  between operations  0.64 us (2%)
    pallas_call x1, Pallas kernels, shards(): pl.pallas_call(kernel, out_shape=(block, block), in_specs=[pl.BlockSpec(m...  38.2 us
    unnamed x2, local copies, waits for them, and re-layouts  1.31 us

profile of v4, /device:TPU:2, one launch (start us, length us, event | category | flops | bytes accessed | tf_op | source)
XLA Modules:
  0.0 40.1 jit_solution(4920696997138542605)
XLA Ops:
  0.6 38.2 %shard_map.68 = (f32[1,16,16,128]{3,2,1,0:T(8,128)S(1)}, f32[1,16,16,128]{3,2,1,0:T(8,128)S(1)}) custom-call(s32[1,16,16,128]{3,2,1,0:T(8,128)} %cls_hbm.1, f32[1,8]{1,0:T(1,128)} %bitcast.3, s32[1,16]{1,0:T(1,128)} %bitcast.4, f32[1,16]{1,0:T(1,128)} %bitcast.5, f32[1,16,16,128]{3,2,1,0:T(8,128)} %guess_hbm.1), custom_call_target="tpu_custom_call" | custom-call | tf_op jit(solution)/shard_map/pallas_call | solution.py:745
  38.8 0.7 %copy.9 = f32[1,16,16,128]{3,2,1,0:T(8,128)} copy(f32[1,16,16,128]{3,2,1,0:T(8,128)S(1)} %get-tuple-element.4) | data formatting | bytes 262144
  39.5 0.7 %copy.10 = f32[1,16,16,128]{3,2,1,0:T(8,128)} copy(f32[1,16,16,128]{3,2,1,0:T(8,128)S(1)} %get-tuple-element.5) | data formatting | bytes 262144

commit v5 on v4

--- a/solution.py
+++ b/solution.py
@@ -525,6 +525,9 @@
     sweep0(vb, u0, g0, c0, 3, 21)
     coarsen0(lambda x: own_residual0(u0, g0, c0, t0, x + 4)[1], w1)
 
+    pack1(w1, sbb1, seb1)
+    send_plan(me, PLAN1, ENDS1, sbb1, rbb1, seb1, reb1, send, recv, 4)
+
     own1 = lanes_of((8, 128)) < 64
 
     def part1(x):
@@ -576,10 +579,7 @@
             src, got, count = PART2[o]
             start_to(me, sbb2.at[pl.ds(src, count)], rbb2.at[pl.ds(got, count)], send.at[9], recv.at[9], o)
 
-    gather(GATHER[:24])
-    pack1(w1, sbb1, seb1)
-    send_plan(me, PLAN1, ENDS1, sbb1, rbb1, seb1, reb1, send, recv, 4)
-    gather(GATHER[24:])
+    gather(GATHER)
     pack0(lambda a, x: u0[x + 4, 0:16, 0:128], 1, sbv, sev)
     send_plan(me, PLANV, EDGE0, sbv, rbv, sev, rev, send, recv, 6)
     for i, buffer in enumerate((rb2, re2, rbk1, rek1)):

time: 40.2 us -> 38.7 us (0.963)
  Pallas kernels: 38.2 us -> 36.6 us
    pallas_call x1, Pallas kernels: 38.2 us -> 36.6 us  [shards(): pl.pallas_call(kernel, out_shape=(block, block), in_specs=[pl.BlockSpec(m...]
where the time goes in v5:
time: 38.7 us; the launch traced here: 38.6 us
  Pallas kernels  36.6 us (95%)
  local copies, waits for them, and re-layouts  1.31 us (3%)
  between operations  0.64 us (2%)
    pallas_call x1, Pallas kernels, shards(): pl.pallas_call(kernel, out_shape=(block, block), in_specs=[pl.BlockSpec(m...  36.6 us
    unnamed x2, local copies, waits for them, and re-layouts  1.31 us

profile of v5, /device:TPU:2, one launch (start us, length us, event | category | flops | bytes accessed | tf_op | source)
XLA Modules:
  0.0 38.6 jit_solution(7709488197130933798)
XLA Ops:
  0.6 36.6 %shard_map.68 = (f32[1,16,16,128]{3,2,1,0:T(8,128)S(1)}, f32[1,16,16,128]{3,2,1,0:T(8,128)S(1)}) custom-call(s32[1,16,16,128]{3,2,1,0:T(8,128)} %cls_hbm.1, f32[1,8]{1,0:T(1,128)} %bitcast.3, s32[1,16]{1,0:T(1,128)} %bitcast.4, f32[1,16]{1,0:T(1,128)} %bitcast.5, f32[1,16,16,128]{3,2,1,0:T(8,128)} %guess_hbm.1), custom_call_target="tpu_custom_call" | custom-call | tf_op jit(solution)/shard_map/pallas_call | solution.py:745
  37.2 0.7 %copy.9 = f32[1,16,16,128]{3,2,1,0:T(8,128)} copy(f32[1,16,16,128]{3,2,1,0:T(8,128)S(1)} %get-tuple-element.4) | data formatting | bytes 262144
  37.9 0.7 %copy.10 = f32[1,16,16,128]{3,2,1,0:T(8,128)} copy(f32[1,16,16,128]{3,2,1,0:T(8,128)S(1)} %get-tuple-element.5) | data formatting | bytes 262144

commit v6 on v5

--- a/solution.py
+++ b/solution.py
@@ -75,7 +75,7 @@
 EDGE0 = {d: (SIDE2[(d[2], d[1])], i, 1) for i, d in enumerate(d for d in DIRS if d[1] and d[2])}
 ENDS1 = {d: ((1 - d[2]) // 2, i, 1) for i, d in enumerate(d for d in DIRS if d[2])}
 NEAR = sorted((offset(d) for d in DIRS), key=lambda o: (-hops(o), o))
-GATHER = sorted((o for o in range(1, N) if o % 4 != 2), key=lambda o: (-hops(o), o))
+GATHER = sorted((o for o in range(1, N) if o % 4 != 2), key=lambda o: (o % 4 == 0, -hops(o), o))
 SLOT = {o: i for i, o in enumerate(GATHER)}
 SLOT[0] = len(GATHER)
 

time: 38.7 us -> 38.1 us (0.984)
  Pallas kernels: 36.6 us -> 36 us
    pallas_call x1, Pallas kernels: 36.6 us -> 36 us  [shards(): pl.pallas_call(kernel, out_shape=(block, block), in_specs=[pl.BlockSpec(m...]
where the time goes in v6:
time: 38.1 us; the launch traced here: 38 us
  Pallas kernels  36 us (94%)
  local copies, waits for them, and re-layouts  1.31 us (3%)
  between operations  0.64 us (2%)
    pallas_call x1, Pallas kernels, shards(): pl.pallas_call(kernel, out_shape=(block, block), in_specs=[pl.BlockSpec(m...  36 us
    unnamed x2, local copies, waits for them, and re-layouts  1.31 us

profile of v6, /device:TPU:2, one launch (start us, length us, event | category | flops | bytes accessed | tf_op | source)
XLA Modules:
  0.0 38.0 jit_solution(14599838362710912994)
XLA Ops:
  0.6 36.0 %shard_map.68 = (f32[1,16,16,128]{3,2,1,0:T(8,128)S(1)}, f32[1,16,16,128]{3,2,1,0:T(8,128)S(1)}) custom-call(s32[1,16,16,128]{3,2,1,0:T(8,128)} %cls_hbm.1, f32[1,8]{1,0:T(1,128)} %bitcast.3, s32[1,16]{1,0:T(1,128)} %bitcast.4, f32[1,16]{1,0:T(1,128)} %bitcast.5, f32[1,16,16,128]{3,2,1,0:T(8,128)} %guess_hbm.1), custom_call_target="tpu_custom_call" | custom-call | tf_op jit(solution)/shard_map/pallas_call | solution.py:745
  36.7 0.7 %copy.9 = f32[1,16,16,128]{3,2,1,0:T(8,128)} copy(f32[1,16,16,128]{3,2,1,0:T(8,128)S(1)} %get-tuple-element.4) | data formatting | bytes 262144
  37.3 0.7 %copy.10 = f32[1,16,16,128]{3,2,1,0:T(8,128)} copy(f32[1,16,16,128]{3,2,1,0:T(8,128)S(1)} %get-tuple-element.5) | data formatting | bytes 262144
